TPU v7x, 32 devices: a whole 2x2x4 slice. The times are simulated.
32 devices in a mesh: pipe: 4 (over y, core), dp: 4 (over z), tensor: 2 (over x).
Axes of the slice: x: 2, y: 2, z: 4, core: 2. Of those that a mesh axis runs over, the one named last changes fastest.
Arguments:
- tokens: bfloat16 [128, 16384], P('dp', 'tensor'), may hold values from -6 to 6
- weight: bfloat16 [4, 16384, 2, 8192], P('pipe', 'tensor', None, 'dp'), may hold values from -0.046875 to 0.046875
- gain: float32 [4, 16384], P('pipe', 'tensor'), may hold values from 0.5 to 1.5
- resident_down: bfloat16 [4, 32, 16, 16384], P('pipe', None, None, 'tensor'), may hold values from -0.046875 to 0.046875
- resident_up: bfloat16 [4, 32, 16, 16384], P('pipe', None, None, 'tensor'), may hold values from -0.23925781 to 0.23925781
- cotangent: bfloat16 [128, 16384], P('dp', 'tensor'), may hold values from -6 to 6
- batch_tenants: int32 [16], P('dp'), may hold values from 0 to 31
- tenant_slots: int32 [32], replicated, may hold values from 0 to 31, each once
Outputs:
- section_out: bfloat16 [4, 128, 16384], P('pipe', 'dp', 'tensor')
- input_grads: bfloat16 [4, 128, 16384], P('pipe', 'dp', 'tensor')
- grad_a: float32 [4, 32, 16, 16384], P('pipe', 'dp', None, 'tensor')
- grad_b: float32 [4, 32, 16, 16384], P('pipe', 'dp', None, 'tensor')
All inputs are finite; a program needn't handle non-finite values.
Results may differ from a plain program's by a relative error of at most 0.018.
Values may be sent and summed in bfloat16 or wider, within the bound.
A program may use at most 384 MiB of HBM per device.

v0:
```python
import jax
import jax.numpy as jnp
from jax import lax
from jax.sharding import PartitionSpec as P

MODEL_WIDTH = 16384


EPS = 1e-05
ADAPTER_SCALE = 2.0


def shifted(block, axis, distance):
    devices = range(lax.axis_size(axis))
    route = [(i - distance, i) for i in devices if i - distance in devices]
    return lax.ppermute(block, axis, route)


def take_block(buffer, position):
    return lax.dynamic_index_in_dim(buffer, position, 0, keepdims=False)


def put_block(buffer, position, value, active):
    previous = lax.dynamic_index_in_dim(buffer, position, 0, keepdims=False)
    return lax.dynamic_update_index_in_dim(buffer, jnp.where(active, value, previous), position, 0)


def local(tokens, weight, gain, resident_down, resident_up, cotangent, batch_tenants, tenant_slots):
    section_count = lax.axis_size("pipe")
    section_id = lax.axis_index("pipe")
    column_id = lax.axis_index("tensor")
    dp_count = lax.axis_size("dp")
    w_block = weight[0]
    scale_row = gain[0]
    down_adapter = resident_down[0]
    up_adapter = resident_up[0]
    width_local = w_block.shape[0]
    tensor_count = w_block.shape[1]
    piece_cols = w_block.shape[2]
    out_cols = tensor_count * piece_cols
    w_flat = w_block.reshape(width_local, out_cols)
    micro_count = batch_tenants.shape[0]
    row_count = tokens.shape[0] // micro_count
    tenant_count = down_adapter.shape[0]
    rank_count = down_adapter.shape[1]
    tick_count = micro_count + section_count - 1
    labels = jnp.arange(tenant_count, dtype=jnp.int32)
    slot_ids = jnp.sum(
        jnp.where(batch_tenants[:, None] == labels[None, :], tenant_slots[None, :], 0), axis=1
    )
    token_blocks = tokens.reshape(micro_count, row_count, width_local)
    cot_blocks = cotangent.reshape(micro_count, row_count, width_local)
    kept_state = jnp.zeros((micro_count, row_count, width_local), jnp.bfloat16)
    kept_normed = jnp.zeros((micro_count, row_count, width_local), jnp.bfloat16)
    kept_branch = jnp.zeros((micro_count, row_count, width_local), jnp.float32)
    kept_inverse = jnp.zeros((micro_count, row_count), jnp.float32)
    kept_low = jnp.zeros((micro_count, row_count, rank_count), jnp.bfloat16)
    outputs = jnp.zeros((micro_count, row_count, width_local), jnp.bfloat16)
    carried = jnp.zeros((row_count, width_local), jnp.bfloat16)
    for step_num in range(tick_count):
        position = step_num - section_id
        active = (position >= 0) & (position < micro_count)
        clipped = jnp.clip(position, 0, micro_count - 1)
        current = jnp.where(section_id == 0, take_block(token_blocks, clipped), carried)
        slot_id = take_block(slot_ids, clipped)
        a_select = take_block(down_adapter, slot_id)
        up_selected = take_block(up_adapter, slot_id)
        wide_state = current.astype(jnp.float32)
        squares = jnp.sum(wide_state * wide_state, axis=1)
        total_sq = lax.psum(squares, "tensor")
        inverse = lax.rsqrt(total_sq / MODEL_WIDTH + EPS)
        normed_input = (wide_state * inverse[:, None] * scale_row[None, :]).astype(jnp.bfloat16)
        low_part = lax.dot_general(
            normed_input, a_select, (((1,), (1,)), ((), ())), preferred_element_type=jnp.float32
        )

        def project(segment, offset, active=active):

            def project_compute(values):
                return jnp.dot(values, w_flat, preferred_element_type=jnp.float32).astype(
                    jnp.bfloat16
                )

            def project_skipped(values):
                return jnp.zeros((values.shape[0], out_cols), jnp.bfloat16)

            return lax.cond(active, project_compute, project_skipped, segment)

        partial_value = project(
            lax.all_gather(normed_input, "dp", axis=0, tiled=True), jnp.int32(0)
        )
        exchanged = lax.all_to_all(partial_value, "dp", split_axis=0, concat_axis=1, tiled=True)
        wide_parts = exchanged.reshape(row_count, dp_count, tensor_count, piece_cols).astype(
            jnp.float32
        )
        summed, low_sum = (
            lax.psum(wide_parts.astype(jnp.bfloat16), "tensor").astype(jnp.float32),
            lax.psum(low_part.astype(jnp.bfloat16), "tensor").astype(jnp.float32),
        )
        frozen_output = lax.dynamic_index_in_dim(summed, column_id, 2, keepdims=False).reshape(
            row_count, width_local
        )
        low_rank_state = low_sum.astype(jnp.bfloat16)
        adapter_branch = frozen_output + ADAPTER_SCALE * jnp.dot(
            low_rank_state, up_selected, preferred_element_type=jnp.float32
        )
        new_state = (wide_state + adapter_branch).astype(jnp.bfloat16)
        kept_state = put_block(kept_state, clipped, current, active)
        kept_normed = put_block(kept_normed, clipped, normed_input, active)
        kept_branch = put_block(kept_branch, clipped, adapter_branch, active)
        kept_inverse = put_block(kept_inverse, clipped, inverse, active)
        kept_low = put_block(kept_low, clipped, low_rank_state, active)
        outputs = put_block(outputs, clipped, new_state, active)
        carried = shifted(new_state, "pipe", 1)
    terms_down = jnp.zeros((micro_count, rank_count, width_local), jnp.float32)
    terms_up = jnp.zeros((micro_count, rank_count, width_local), jnp.float32)
    grads_out = jnp.zeros((micro_count, row_count, width_local), jnp.bfloat16)
    carried = jnp.zeros((row_count, width_local), jnp.bfloat16)
    for step_num in range(tick_count):
        position = step_num - (section_count - 1 - section_id)
        active = (position >= 0) & (position < micro_count)
        clipped = jnp.clip(position, 0, micro_count - 1)
        incoming_state = jnp.where(
            section_id == section_count - 1, take_block(cot_blocks, clipped), carried
        )
        slot_id = take_block(slot_ids, clipped)
        a_select = take_block(down_adapter, slot_id)
        up_selected = take_block(up_adapter, slot_id)
        current = take_block(kept_state, clipped)
        normed_input = take_block(kept_normed, clipped)
        adapter_branch = take_block(kept_branch, clipped)
        inverse = take_block(kept_inverse, clipped)
        low_rank_state = take_block(kept_low, clipped)
        grad_wide = incoming_state.astype(jnp.float32)
        full_grad = lax.all_gather(incoming_state, "tensor", axis=1, tiled=True)
        routed = lax.all_to_all(
            full_grad.reshape(row_count, tensor_count, dp_count, piece_cols),
            "dp",
            split_axis=2,
            concat_axis=0,
            tiled=True,
        )
        spread_grad = routed.reshape(dp_count * row_count, out_cols)

        def back_rows(offset, amount, active=active, spread_grad=spread_grad):

            def back_compute(values):
                return lax.dot_general(
                    values, w_flat, (((1,), (1,)), ((), ())), preferred_element_type=jnp.float32
                )

            def back_skipped(values):
                return jnp.zeros((values.shape[0], width_local), jnp.float32)

            return lax.cond(active, back_compute, back_skipped, spread_grad)

        frozen_backward = lax.psum_scatter(
            back_rows(jnp.int32(0), row_count * lax.axis_size("dp")).astype(jnp.bfloat16),
            "dp",
            scatter_dimension=0,
            tiled=True,
        ).astype(jnp.float32)
        low_part = lax.dot_general(
            incoming_state,
            up_selected,
            (((1,), (1,)), ((), ())),
            preferred_element_type=jnp.float32,
        )
        stat_part = jnp.sum(grad_wide * adapter_branch, axis=1)
        low_sum, statistic = lax.psum((low_part, stat_part), "tensor")
        low_grad = low_sum.astype(jnp.bfloat16)
        normed_gradient = frozen_backward + ADAPTER_SCALE * jnp.dot(
            low_grad, a_select, preferred_element_type=jnp.float32
        )
        wide_state = current.astype(jnp.float32)
        change = (
            grad_wide
            + inverse[:, None] * scale_row[None, :] * normed_gradient
            - wide_state * (inverse * inverse * statistic / MODEL_WIDTH)[:, None]
        )
        new_grad = change.astype(jnp.bfloat16)
        down_term = ADAPTER_SCALE * lax.dot_general(
            low_grad, normed_input, (((0,), (0,)), ((), ())), preferred_element_type=jnp.float32
        )
        up_term = ADAPTER_SCALE * lax.dot_general(
            low_rank_state,
            incoming_state,
            (((0,), (0,)), ((), ())),
            preferred_element_type=jnp.float32,
        )
        terms_down = put_block(terms_down, clipped, down_term, active)
        terms_up = put_block(terms_up, clipped, up_term, active)
        grads_out = put_block(grads_out, clipped, new_grad, active)
        carried = shifted(new_grad, "pipe", -1)
    slot_hot = (slot_ids[:, None] == labels[None, :]).astype(jnp.float32)
    grad_a = jnp.einsum("ms,mrw->srw", slot_hot, terms_down, precision=lax.Precision.HIGHEST)
    grad_b = jnp.einsum("ms,mrw->srw", slot_hot, terms_up, precision=lax.Precision.HIGHEST)
    summed_a, summed_b = (
        lax.psum_scatter(grad_a.astype(jnp.bfloat16), "dp", scatter_dimension=0, tiled=True).astype(
            jnp.float32
        ),
        lax.psum_scatter(grad_b.astype(jnp.bfloat16), "dp", scatter_dimension=0, tiled=True).astype(
            jnp.float32
        ),
    )
    section_out = outputs.reshape(1, micro_count * row_count, width_local)
    input_grads = grads_out.reshape(1, micro_count * row_count, width_local)
    return (section_out, input_grads, summed_a[None], summed_b[None])


def solution(mesh):
    placed = (
        P("dp", "tensor"),
        P("pipe", "tensor", None, "dp"),
        P("pipe", "tensor"),
        P("pipe", None, None, "tensor"),
        P("pipe", None, None, "tensor"),
        P("dp", "tensor"),
        P("dp"),
        P(),
    )
    return jax.shard_map(
        local,
        mesh=mesh,
        in_specs=placed,
        out_specs=(
            P("pipe", "dp", "tensor"),
            P("pipe", "dp", "tensor"),
            P("pipe", "dp", None, "tensor"),
            P("pipe", "dp", None, "tensor"),
        ),
        check_vma=False,
    )
```

profile of v0, /device:TPU:0, one launch (start us, length us, event | category | flops | bytes accessed | tf_op | source)
XLA Modules:
  0.0 1615.4 jit_solution(2337172809076344368)
XLA Ops:
  15.1 15.7 all_gather.42
  30.8 44.3 %copy.178 = bf16[1024,8,2,2048]{3,1,2,0:T(8,128)(2,1)} copy(bf16[1024,8,2,2048]{3,2,1,0:T(2,128)(2,1)} %bitcast.312) | data formatting | bytes 134217728
  75.1 24.2 %conditional.14 = (bf16[32,4096]{1,0:T(8,128)(2,1)}) conditional(s32[]{:T(128)} %convert_element_type.367, () %tuple.92, (bf16[32,8192]{1,0:T(8,128)(2,1)S(1)}, bf16[8192,4096]{1,0:T(8,128)(2,1)}) %tuple.93), branch_computations={%region_2.3_spmd, %region_3.4_spmd} | conditional | flops 2147614720 | bytes 67895304 | solution.py:87
  75.2 24.2 %convolution_convert_fusion = bf16[32,4096]{1,0:T(8,128)(2,1)} fusion(bf16[32,8192]{1,0:T(8,128)(2,1)S(1)} %get-tuple-element.98, bf16[8192,4096]{1,0:T(8,128)(2,1)} %get-tuple-element.99), kind=kOutput, calls=%fused_computation | convolution fusion | flops 2147614720 | bytes 67895296 | tf_op jit(solution)/shard_map/cond/branch_1_fun/dot_general | solution.py:80
  146.6 17.1 %all_gather.43 = bf16[32,8192]{1,0:T(8,128)(2,1)} all-gather(bf16[8,8192]{1,0:T(8,128)(2,1)S(1)} %get-tuple-element.220), channel_id=1, replica_groups=mesh['pipe'=4,'dp'=4,'tensor'=2] {'dp'}, dimensions={0}, use_global_device_ids=true | all-gather | bytes 655360 | tf_op jit(solution)/shard_map/all_gather | solution.py:90
  163.7 25.3 %conditional.15 = (bf16[32,4096]{1,0:T(8,128)(2,1)}) conditional(s32[]{:T(128)} %convert_element_type.376, () %tuple.94, (bf16[32,8192]{1,0:T(8,128)(2,1)}, bf16[8192,4096]{1,0:T(8,128)(2,1)}) %tuple.95), branch_computations={%region_9.10_spmd, %region_10.11_spmd} | conditional | flops 2147614720 | bytes 67895304 | solution.py:87
  163.7 25.3 %convolution_convert_fusion.1 = bf16[32,4096]{1,0:T(8,128)(2,1)} fusion(bf16[32,8192]{1,0:T(8,128)(2,1)} %get-tuple-element.100, bf16[8192,4096]{1,0:T(8,128)(2,1)} %get-tuple-element.104), kind=kOutput, calls=%fused_computation.1 | convolution fusion | flops 2147614720 | bytes 67895296 | tf_op jit(solution)/shard_map/cond/branch_1_fun/dot_general | solution.py:80
  238.0 17.2 %all_gather.44 = bf16[32,8192]{1,0:T(8,128)(2,1)} all-gather(bf16[8,8192]{1,0:T(8,128)(2,1)S(1)} %get-tuple-element.218), channel_id=1, replica_groups=mesh['pipe'=4,'dp'=4,'tensor'=2] {'dp'}, dimensions={0}, use_global_device_ids=true | all-gather | bytes 655360 | tf_op jit(solution)/shard_map/all_gather | solution.py:90
  255.1 25.5 %conditional.16 = (bf16[32,4096]{1,0:T(8,128)(2,1)}) conditional(s32[]{:T(128)} %convert_element_type.382, () %tuple.96, (bf16[32,8192]{1,0:T(8,128)(2,1)}, bf16[8192,4096]{1,0:T(8,128)(2,1)}) %tuple.97), branch_computations={%region_15.16_spmd, %region_16.17_spmd} | conditional | flops 2147614720 | bytes 67895304 | solution.py:87
  255.3 25.3 %convolution_convert_fusion.2 = bf16[32,4096]{1,0:T(8,128)(2,1)} fusion(bf16[32,8192]{1,0:T(8,128)(2,1)} %get-tuple-element.106, bf16[8192,4096]{1,0:T(8,128)(2,1)} %get-tuple-element.107), kind=kOutput, calls=%fused_computation.2 | convolution fusion | flops 2147614720 | bytes 67895296 | tf_op jit(solution)/shard_map/cond/branch_1_fun/dot_general | solution.py:80
  331.5 17.2 %all_gather.45 = bf16[32,8192]{1,0:T(8,128)(2,1)} all-gather(bf16[8,8192]{1,0:T(8,128)(2,1)S(1)} %get-tuple-element.216), channel_id=1, replica_groups=mesh['pipe'=4,'dp'=4,'tensor'=2] {'dp'}, dimensions={0}, use_global_device_ids=true | all-gather | bytes 655360 | tf_op jit(solution)/shard_map/all_gather | solution.py:90
  348.7 25.3 %conditional.17 = (bf16[32,4096]{1,0:T(8,128)(2,1)}) conditional(s32[]{:T(128)} %convert_element_type.388, () %tuple.98, (bf16[32,8192]{1,0:T(8,128)(2,1)}, bf16[8192,4096]{1,0:T(8,128)(2,1)}) %tuple.99), branch_computations={%region_21.22_spmd, %region_22.23_spmd} | conditional | flops 2147614720 | bytes 67895304 | solution.py:87
  348.7 25.3 %convolution_convert_fusion.3 = bf16[32,4096]{1,0:T(8,128)(2,1)} fusion(bf16[32,8192]{1,0:T(8,128)(2,1)} %get-tuple-element.108, bf16[8192,4096]{1,0:T(8,128)(2,1)} %get-tuple-element.112), kind=kOutput, calls=%fused_computation.3 | convolution fusion | flops 2147614720 | bytes 67895296 | tf_op jit(solution)/shard_map/cond/branch_1_fun/dot_general | solution.py:80
  424.9 17.2 %all_gather.46 = bf16[32,8192]{1,0:T(8,128)(2,1)} all-gather(bf16[8,8192]{1,0:T(8,128)(2,1)S(1)} %get-tuple-element.214), channel_id=1, replica_groups=mesh['pipe'=4,'dp'=4,'tensor'=2] {'dp'}, dimensions={0}, use_global_device_ids=true | all-gather | bytes 655360 | tf_op jit(solution)/shard_map/all_gather | solution.py:90
  463.1 42.3 %all-reduce.23.cloned.1.call-done = bf16[8,4,2,2048]{3,2,0,1:T(2,128)(2,1)} async-done(((bf16[8,4,2,2048]{3,2,0,1:T(2,128)(2,1)}), bf16[8,4,2,2048]{3,2,0,1:T(2,128)(2,1)}) %all-reduce.23.cloned.1.call-update) | async-done | bytes 262160 | tf_op jit(solution)/shard_map/psum | solution.py:97
  518.0 17.0 %all_gather.47 = bf16[32,8192]{1,0:T(8,128)(2,1)} all-gather(bf16[8,8192]{1,0:T(8,128)(2,1)S(1)} %get-tuple-element.212), channel_id=1, replica_groups=mesh['pipe'=4,'dp'=4,'tensor'=2] {'dp'}, dimensions={0}, use_global_device_ids=true | all-gather | bytes 655360 | tf_op jit(solution)/shard_map/all_gather | solution.py:90
  558.0 40.8 %all-reduce.25.cloned.1.call-done = bf16[8,4,2,2048]{3,2,0,1:T(2,128)(2,1)} async-done(((bf16[8,4,2,2048]{3,2,0,1:T(2,128)(2,1)}), bf16[8,4,2,2048]{3,2,0,1:T(2,128)(2,1)}) %all-reduce.25.cloned.1.call-update) | async-done | bytes 262160 | tf_op jit(solution)/shard_map/psum | solution.py:97
  612.6 16.4 %all_gather.48 = bf16[32,8192]{1,0:T(8,128)(2,1)S(1)} all-gather(bf16[8,8192]{1,0:T(8,128)(2,1)S(1)} %get-tuple-element.210), channel_id=1, replica_groups=mesh['pipe'=4,'dp'=4,'tensor'=2] {'dp'}, dimensions={0}, use_global_device_ids=true | all-gather | bytes 655360 | tf_op jit(solution)/shard_map/all_gather | solution.py:90
  651.0 31.9 %all-reduce.27.cloned.1.call-done = bf16[8,4,2,2048]{3,2,0,1:T(2,128)(2,1)} async-done(((bf16[8,4,2,2048]{3,2,0,1:T(2,128)(2,1)}), bf16[8,4,2,2048]{3,2,0,1:T(2,128)(2,1)}) %all-reduce.27.cloned.1.call-update) | async-done | bytes 262160 | tf_op jit(solution)/shard_map/psum | solution.py:97
  714.9 37.8 %reduce-scatter.14.cloned.1.call-done = bf16[8,8192]{1,0:T(8,128)(2,1)} async-done(((bf16[32,8192]{1,0:T(8,128)(2,1)}), bf16[8,8192]{1,0:T(8,128)(2,1)}) %reduce-scatter.14.cloned.1.call-update) | async-done | bytes 131088 | tf_op jit(solution)/shard_map/reduce_scatter | solution.py:157
  784.5 43.5 %reduce-scatter.16.cloned.1.call-done = bf16[8,8192]{1,0:T(8,128)(2,1)} async-done(((bf16[32,8192]{1,0:T(8,128)(2,1)}), bf16[8,8192]{1,0:T(8,128)(2,1)}) %reduce-scatter.16.cloned.1.call-update) | async-done | bytes 131088 | tf_op jit(solution)/shard_map/reduce_scatter | solution.py:157
  886.6 42.4 %reduce-scatter.18.cloned.1.call-done = bf16[8,8192]{1,0:T(8,128)(2,1)} async-done(((bf16[32,8192]{1,0:T(8,128)(2,1)}), bf16[8,8192]{1,0:T(8,128)(2,1)}) %reduce-scatter.18.cloned.1.call-update) | async-done | bytes 131088 | tf_op jit(solution)/shard_map/reduce_scatter | solution.py:157
  970.6 29.5 %conditional.24 = (bf16[32,8192]{1,0:T(8,128)(2,1)}) conditional(s32[]{:T(128)} %convert_element_type.436, () %tuple.112, (bf16[4,8,2,1,2048]{4,1,3,0,2:T(8,128)(2,1)}, bf16[8192,4096]{1,0:T(8,128)(2,1)}) %tuple.276), branch_computations={%region_61.62_spmd, %region_62.63_spmd} | conditional | flops 2147483648 | bytes 68943880 | solution.py:155
  972.6 27.5 %fusion.328 = bf16[32,8192]{1,0:T(8,128)(2,1)} fusion(bf16[32,4096]{1,0:T(8,128)(2,1)} %bitcast.894, bf16[8192,4096]{1,0:T(8,128)(2,1)} %get-tuple-element.126), kind=kOutput, calls=%fused_computation.572 | convolution fusion | flops 2147483648 | bytes 67895296 | tf_op jit(solution)/shard_map/cond/branch_1_fun/dot_general | solution.py:148
  1063.5 29.5 %conditional.25 = (bf16[32,8192]{1,0:T(8,128)(2,1)}) conditional(s32[]{:T(128)} %convert_element_type.444, () %tuple.114, (bf16[4,8,2,1,2048]{4,1,3,0,2:T(8,128)(2,1)}, bf16[8192,4096]{1,0:T(8,128)(2,1)}) %tuple.277), branch_computations={%region_67.68_spmd, %region_68.69_spmd} | conditional | flops 2147483648 | bytes 68943880 | solution.py:155
  1065.6 27.5 %fusion.329 = bf16[32,8192]{1,0:T(8,128)(2,1)} fusion(bf16[32,4096]{1,0:T(8,128)(2,1)} %bitcast.895, bf16[8192,4096]{1,0:T(8,128)(2,1)} %get-tuple-element.128), kind=kOutput, calls=%fused_computation.573 | convolution fusion | flops 2147483648 | bytes 67895296 | tf_op jit(solution)/shard_map/cond/branch_1_fun/dot_general | solution.py:148
  1156.0 29.5 %conditional.26 = (bf16[32,8192]{1,0:T(8,128)(2,1)}) conditional(s32[]{:T(128)} %convert_element_type.452, () %tuple.116, (bf16[4,8,2,1,2048]{4,1,3,0,2:T(8,128)(2,1)}, bf16[8192,4096]{1,0:T(8,128)(2,1)}) %tuple.278), branch_computations={%region_73.74_spmd, %region_74.75_spmd} | conditional | flops 2147483648 | bytes 68943880 | solution.py:155
  1158.0 27.5 %fusion.330 = bf16[32,8192]{1,0:T(8,128)(2,1)} fusion(bf16[32,4096]{1,0:T(8,128)(2,1)} %bitcast.896, bf16[8192,4096]{1,0:T(8,128)(2,1)} %get-tuple-element.130), kind=kOutput, calls=%fused_computation.574 | convolution fusion | flops 2147483648 | bytes 67895296 | tf_op jit(solution)/shard_map/cond/branch_1_fun/dot_general | solution.py:148
  1247.7 28.7 %conditional.27 = (bf16[32,8192]{1,0:T(8,128)(2,1)S(1)}) conditional(s32[]{:T(128)} %convert_element_type.460, () %tuple.118, (bf16[4,8,2,1,2048]{4,1,3,0,2:T(8,128)(2,1)S(1)}, bf16[8192,4096]{1,0:T(8,128)(2,1)}) %tuple.272), branch_computations={%region_79.80_spmd, %region_80.81_spmd} | conditional | flops 2147483648 | bytes 68943880 | solution.py:155
  1248.1 28.3 %fusion.331 = bf16[32,8192]{1,0:T(8,128)(2,1)S(1)} fusion(bf16[32,4096]{1,0:T(8,128)(2,1)S(1)} %bitcast.897, bf16[8192,4096]{1,0:T(8,128)(2,1)} %get-tuple-element.132), kind=kOutput, calls=%fused_computation.575 | convolution fusion | flops 2147483648 | bytes 67895296 | tf_op jit(solution)/shard_map/cond/branch_1_fun/dot_general | solution.py:148
  1403.1 53.0 %reduce-scatter.28.cloned.1.call-done = bf16[8,131072]{1,0:T(8,128)(2,1)} async-done(((bf16[32,131072]{1,0:T(8,128)(2,1)}), bf16[8,131072]{1,0:T(8,128)(2,1)}) %reduce-scatter.28.cloned.1.call-update) | async-done | bytes 2097168
  1460.9 142.8 %reduce-scatter.30.cloned.1.call-done = bf16[8,131072]{1,0:T(8,128)(2,1)} async-done(((bf16[32,131072]{1,0:T(8,128)(2,1)}), bf16[8,131072]{1,0:T(8,128)(2,1)}) %reduce-scatter.30.cloned.1.call-update) | async-done | bytes 2097168
  (437 shorter events, 768.7 us)
Async XLA Ops:
  104.5 29.9 %all-reduce.15.cloned.1.call-start = ((), (), s32[]{:S(2)}) async-start(), calls=%async_computation.23 | async-start | bytes 524288 | tf_op jit(solution)/shard_map/psum | solution.py:97
  189.0 13.3 all-to-all-start.1
  193.4 31.3 %all-reduce.17.cloned.1.call-start = ((), (), s32[]{:S(2)}) async-start(), calls=%async_computation.24 | async-start | bytes 524288 | tf_op jit(solution)/shard_map/psum | solution.py:97
  280.6 13.3 all-to-all-start.2
  285.0 33.2 %all-reduce.19.cloned.1.call-start = ((), (), s32[]{:S(2)}) async-start(), calls=%async_computation.25 | async-start | bytes 524288 | tf_op jit(solution)/shard_map/psum | solution.py:97
  374.0 13.3 all-to-all-start.3
  378.4 33.2 %all-reduce.21.cloned.1.call-start = ((), (), s32[]{:S(2)}) async-start(), calls=%async_computation.26 | async-start | bytes 524288 | tf_op jit(solution)/shard_map/psum | solution.py:97
  447.6 57.8 %all-reduce.23.cloned.1.call-start = ((), (), s32[]{:S(2)}) async-start(), calls=%async_computation.27 | async-start | bytes 524288 | tf_op jit(solution)/shard_map/psum | solution.py:97
  535.7 13.7 all-to-all-start.5
  540.1 58.7 %all-reduce.25.cloned.1.call-start = ((), (), s32[]{:S(2)}) async-start(), calls=%async_computation.28 | async-start | bytes 524288 | tf_op jit(solution)/shard_map/psum | solution.py:97
  629.9 13.5 all-to-all-start.6
  634.1 48.8 %all-reduce.27.cloned.1.call-start = ((), (), s32[]{:S(2)}) async-start(), calls=%async_computation.29 | async-start | bytes 524288 | tf_op jit(solution)/shard_map/psum | solution.py:97
  698.6 54.2 %reduce-scatter.14.cloned.1.call-start = ((), (), s32[]{:S(2)}) async-start(), calls=%async_computation.30 | async-start | bytes 655360 | tf_op jit(solution)/shard_map/reduce_scatter | solution.py:157
  764.7 12.0 all-to-all-start.8
  768.1 59.8 %reduce-scatter.16.cloned.1.call-start = ((), (), s32[]{:S(2)}) async-start(), calls=%async_computation.31 | async-start | bytes 655360 | tf_op jit(solution)/shard_map/reduce_scatter | solution.py:157
  829.8 23.5 %collective-permute-start.7 = (bf16[8,8192]{1,0:T(8,128)(2,1)}, bf16[8,8192]{1,0:T(8,128)(2,1)}, u32[]{:S(2)}, u32[]{:S(2)}) collective-permute-start(bf16[8,8192]{1,0:T(8,128)(2,1)} %get-tuple-element.313), channel_id=1, source_target_pairs={{8,0},{16,8},{24,16},{9,1},{17,9},{25,17},{10,2},{18,10},{26,18},{... | collective-permute-start | bytes 393224 | tf_op jit(solution)/shard_map/ppermute | solution.py:16
  862.8 13.5 all-to-all-start.9
  866.8 62.2 %reduce-scatter.18.cloned.1.call-start = ((), (), s32[]{:S(2)}) async-start(), calls=%async_computation.32 | async-start | bytes 655360 | tf_op jit(solution)/shard_map/reduce_scatter | solution.py:157
  931.1 14.8 collective-permute-start.8
  955.4 13.5 all-to-all-start.10
  959.4 62.2 %reduce-scatter.20.cloned.1.call-start = ((), (), s32[]{:S(2)}) async-start(), calls=%async_computation.33 | async-start | bytes 655360 | tf_op jit(solution)/shard_map/reduce_scatter | solution.py:157
  1023.7 15.2 collective-permute-start.9
  1048.3 13.5 all-to-all-start.11
  1052.4 62.1 %reduce-scatter.22.cloned.1.call-start = ((), (), s32[]{:S(2)}) async-start(), calls=%async_computation.34 | async-start | bytes 655360 | tf_op jit(solution)/shard_map/reduce_scatter | solution.py:157
  1116.6 14.8 collective-permute-start.10
  1140.8 13.5 all-to-all-start.12
  1144.8 60.7 %reduce-scatter.24.cloned.1.call-start = ((), (), s32[]{:S(2)}) async-start(), calls=%async_computation.35 | async-start | bytes 655360 | tf_op jit(solution)/shard_map/reduce_scatter | solution.py:157
  1207.6 14.8 collective-permute-start.11
  1231.9 14.8 all-to-all-start.13
  1235.9 165.2 %reduce-scatter.26.cloned.1.call-start = ((), (), s32[]{:S(2)}) async-start(), calls=%async_computation.36 | async-start | bytes 655360 | tf_op jit(solution)/shard_map/reduce_scatter | solution.py:157
  1277.2 178.9 %reduce-scatter.28.cloned.1.call-start = ((), (), s32[]{:S(2)}) async-start(), calls=%async_computation.37 | async-start | bytes 10485760
  1311.1 292.5 %reduce-scatter.30.cloned.1.call-start = ((), (), s32[]{:S(2)}) async-start(), calls=%async_computation.38 | async-start | bytes 10485760
  (45 other events, 1120.0 us)
Sparse Core Ops, SparseCore 0:
  112.3 22.0 all-reduce.14
  204.3 20.3 all-reduce.16
  295.9 22.2 all-reduce.18
  389.3 22.2 all-reduce.20
  456.5 48.8 all-reduce.22
  551.4 47.3 all-reduce.24
  644.3 38.4 all-reduce.26
  707.1 45.6 reduce-scatter.13
  778.4 49.4 reduce-scatter.15
  879.0 50.0 reduce-scatter.17
  1000.3 21.3 reduce-scatter.19
  1093.2 21.2 reduce-scatter.21
  1185.7 19.8 reduce-scatter.23
  1277.3 21.9 reduce-scatter.25
  1311.2 144.7 reduce-scatter.27
  1458.4 145.2 reduce-scatter.29
where the time goes:
time: 1630 us; the launch traced here: 1620 us
  waiting for transfers between devices  623 us (38%)
  local copies, waits for them, and re-layouts  284 us (17%)
  matrix products  283 us (17%)
  blocking collectives  268 us (16%)
  starting transfers between devices  76.1 us (5%)
  between operations  42.2 us (3%)
  other arithmetic  37.1 us (2%)
    unnamed x18, waiting for transfers between devices  196 us
    reduce_scatter x7, waiting for transfers between devices, local(): lax.psum_scatter(back_rows(jnp.int32(0), row_count * lax.axis_size('dp'))...  163 us
    psum x7, waiting for transfers between devices, local(): lax.psum(wide_parts.astype(jnp.bfloat16), 'tensor').astype(jnp.float32)  162 us
    dynamic_update_slice x21, local copies, waits for them, and re-layouts, put_block(): lax.dynamic_update_index_in_dim(buffer, jnp.where(active, value, previous...  127 us
    all_gather x7, blocking collectives, local(): lax.all_gather(normed_input, 'dp', axis=0, tiled=True)  118 us
    dot_general x4, matrix products, back_compute(): lax.dot_general(values, w_flat, (((1,), (1,)), ((), ())), preferred_eleme...  111 us
    dot_general x4, matrix products, project_compute(): jnp.dot(values, w_flat, preferred_element_type=jnp.float32)  100 us
    unnamed x75, local copies, waits for them, and re-layouts  75.4 us
  transfers between devices with their start and end apart: 42, of which 30 were waited for; matrix products, arithmetic and copies ran while one was open for 15% of the time, Pallas kernels for 0%

commit v1 on v0

v1 whole, which is shorter than its diff:
```python
import jax
import jax.numpy as jnp
from jax import lax
from jax.sharding import PartitionSpec as P

EPS = 1e-05
ADAPTER_SCALE = 2.0
F32 = jnp.float32
BF16 = jnp.bfloat16


def make_local(section_count, dp_count, tensor_count):
    axes = ("pipe", "dp", "tensor")

    def index_of(section, dp, tensor):
        return (section * dp_count + dp) * tensor_count + tensor

    def send(value, source, target, dp_shift=0, tensor_shift=0):
        pairs = [
            (
                index_of(source, d, t),
                index_of(target, (d + dp_shift) % dp_count, (t + tensor_shift) % tensor_count),
            )
            for d in range(dp_count)
            for t in range(tensor_count)
        ]
        return lax.ppermute(value, axes, pairs)

    def local(tokens, weight, gain, resident_down, resident_up, cotangent, batch_tenants, tenant_slots):
        section_id = lax.axis_index("pipe")
        dp_id = lax.axis_index("dp")
        tensor_id = lax.axis_index("tensor")
        w_block = weight[0]
        gain_row = gain[0]
        width_local, _, piece_cols = w_block.shape
        w_flat = w_block.reshape(width_local, tensor_count * piece_cols)
        model_width = width_local * tensor_count
        own_rows = tokens.shape[0]
        rows = own_rows * dp_count
        slots, rank = resident_down.shape[1:3]
        micro_rows = own_rows // batch_tenants.shape[0]
        own_slots = slots // dp_count
        down_flat = resident_down[0].reshape(slots * rank, width_local)
        up_flat = resident_up[0].reshape(slots * rank, width_local)
        first_col = dp_id * piece_cols

        def own_cols(array):
            return lax.dynamic_slice_in_dim(array, first_col, piece_cols, array.ndim - 1)

        down_cols = own_cols(down_flat)
        up_cols = own_cols(up_flat)
        gain_cols = own_cols(gain_row)
        all_tenants = lax.all_gather(batch_tenants, "dp", axis=0, tiled=True)
        labels = jnp.arange(slots, dtype=jnp.int32)
        slot_ids = jnp.sum(
            jnp.where(all_tenants[:, None] == labels[None, :], tenant_slots[None, :], 0), axis=1
        )
        row_slots = jnp.repeat(slot_ids, micro_rows)
        picks = row_slots[:, None] == labels[None, :]
        lane_slot = jnp.arange(slots * rank, dtype=jnp.int32) // rank
        lane_rank = jnp.arange(slots * rank, dtype=jnp.int32) % rank
        lane_pick = row_slots[:, None] == lane_slot[None, :]
        fold = (lane_rank[:, None] == jnp.arange(rank)[None, :]).astype(F32)
        first_lane = dp_id * own_slots * rank

        def narrow(terms):
            kept = jnp.where(lane_pick, terms, 0.0).reshape(rows, slots, rank)
            return jnp.sum(kept, axis=1).T

        def spread(values):
            wide = jnp.tile(values, (1, slots))
            return jnp.where(lane_pick, wide, jnp.zeros((), values.dtype))

        def gather_dp(parts_by_shift, axis):
            stacked = jnp.stack(parts_by_shift)
            order = [
                lax.dynamic_index_in_dim(stacked, (dp_id - d) % dp_count, 0, keepdims=False)
                for d in range(dp_count)
            ]
            return jnp.concatenate(order, axis=axis)

        def gather_tensor(parts_by_shift):
            stacked = jnp.stack(parts_by_shift)
            order = [
                lax.dynamic_index_in_dim(stacked, (tensor_id - t) % tensor_count, 0, keepdims=False)
                for t in range(tensor_count)
            ]
            return jnp.concatenate(order, axis=1)

        def sum_tensor(value, section):
            total = value
            for shift in range(1, tensor_count):
                total = total + send(value, section, section, 0, shift)
            return total

        def sum_dp(value, section):
            total = value
            for shift in range(1, dp_count):
                total = total + send(value, section, section, shift, 0)
            return total

        def dp_all(value, source, target):
            head = value if source == target else send(value, source, target)
            return [head] + [send(value, source, target, s) for s in range(1, dp_count)]

        def rows_from_cols(value, section):
            parts = []
            for shift in range(dp_count):
                at = ((dp_id + shift) % dp_count) * own_rows
                block = lax.dynamic_slice_in_dim(value, at, own_rows, 0)
                parts.append(block if shift == 0 else send(block, section, section, shift))
            return gather_dp(parts, 1)

        def own_row_block(value):
            return lax.dynamic_slice_in_dim(value, dp_id * own_rows, own_rows, 0)

        last = section_count - 1
        state = gather_dp(dp_all(tokens, 0, 0), 0)
        cot_full = gather_dp(dp_all(cotangent, last, last), 0)
        kept = []
        out_rows = [None] * section_count
        for k in range(section_count):
            wide = state.astype(F32)
            squares = sum_tensor(jnp.sum(wide * wide, axis=1)[None, :], k)
            scaled = (wide * gain_row[None, :]).astype(BF16)
            low_part = narrow(
                lax.dot_general(scaled, down_flat, (((1,), (1,)), ((), ())), preferred_element_type=F32)
            )
            low_raw = sum_tensor(low_part, k)
            product = jnp.dot(scaled, w_flat, preferred_element_type=F32).astype(BF16)
            blocks = product.reshape(rows, tensor_count, piece_cols)
            base = jnp.zeros((rows, piece_cols), F32)
            for shift in range(tensor_count):
                block = lax.dynamic_index_in_dim(
                    blocks, (tensor_id + shift) % tensor_count, 1, keepdims=False
                )
                if shift:
                    block = send(block, k, k, 0, shift)
                base = base + block.astype(F32)
            inverse = lax.rsqrt(squares / model_width + EPS)
            low = (low_raw * inverse).astype(BF16).T
            inverse = inverse[0]
            branch = base * inverse[:, None] + ADAPTER_SCALE * jnp.dot(
                spread(low), up_cols, preferred_element_type=F32
            )
            state_cols = own_cols(state).astype(F32)
            new_cols = (state_cols + branch).astype(BF16)
            kept.append((state, inverse, low, branch, state_cols))
            if k < last:
                state = gather_dp(dp_all(new_cols, k, k + 1), 1)
                out_rows[k] = send(own_row_block(state), k + 1, k)
            else:
                out_rows[k] = rows_from_cols(new_cols, k)
        grad_rows = [None] * section_count
        finals = [None] * section_count
        grad_cols = own_cols(cot_full)
        grad_parts = [grad_cols] + [send(grad_cols, last, last, 0, s) for s in range(1, tensor_count)]
        for k in range(last, -1, -1):
            state, inverse, low, branch, state_cols = kept[k]
            grad_cols = grad_parts[0]
            grad_wide = grad_cols.astype(F32)
            low_part = narrow(
                lax.dot_general(grad_cols, up_cols, (((1,), (1,)), ((), ())), preferred_element_type=F32)
            )
            stat_part = jnp.sum(grad_wide * branch, axis=1)
            small = sum_dp(sum_tensor(jnp.concatenate([low_part, stat_part[None, :]], axis=0), k), k)
            incoming = gather_tensor(grad_parts)
            partial = lax.dot_general(
                incoming, w_flat, (((1,), (1,)), ((), ())), preferred_element_type=F32
            ).astype(BF16)
            frozen = jnp.zeros((rows, piece_cols), F32)
            for shift in range(dp_count):
                at = ((dp_id + shift) % dp_count) * piece_cols
                block = lax.dynamic_slice_in_dim(partial, at, piece_cols, 1)
                if shift:
                    block = send(block, k, k, shift)
                frozen = frozen + block.astype(F32)
            if k == last:
                grad_full = cot_full
            else:
                grad_full = gather_dp(dp_all(grad_cols, k, k), 1)
                grad_rows[k + 1] = send(own_row_block(grad_full), k, k + 1)
            low_grad = small[:rank].astype(BF16).T
            statistic = small[rank]
            dnormed = frozen + ADAPTER_SCALE * jnp.dot(
                spread(low_grad), down_cols, preferred_element_type=F32
            )
            change = (
                grad_wide
                + inverse[:, None] * gain_cols[None, :] * dnormed
                - state_cols * (inverse * inverse * statistic / model_width)[:, None]
            )
            new_grad = change.astype(BF16)
            finals[k] = (state, inverse, low, low_grad, grad_full)
            if k > 0:
                grad_parts = [send(new_grad, k, k - 1, 0, s) for s in range(tensor_count)]
            else:
                grad_rows[0] = rows_from_cols(new_grad, 0)

        def mine(values):
            picked = values[0]
            for k in range(1, section_count):
                picked = jnp.where(section_id == k, values[k], picked)
            return picked

        state, inverse, low, low_grad, grad_full = [mine(list(v)) for v in zip(*finals)]
        normed = (state.astype(F32) * inverse[:, None] * gain_row[None, :]).astype(BF16)
        lanes = own_slots * rank

        def own_lanes(values):
            return lax.dynamic_slice_in_dim(spread(values), first_lane, lanes, 1)

        def adapter_grad(left, right):
            total = ADAPTER_SCALE * lax.dot_general(
                own_lanes(left), right, (((0,), (0,)), ((), ())), preferred_element_type=F32
            )
            return total.reshape(1, own_slots, rank, width_local)

        grad_a = adapter_grad(low_grad, normed)
        grad_b = adapter_grad(low, grad_full)
        return mine(out_rows)[None], mine(grad_rows)[None], grad_a, grad_b

    return local


def solution(mesh):
    placed = (
        P("dp", "tensor"),
        P("pipe", "tensor", None, "dp"),
        P("pipe", "tensor"),
        P("pipe", None, None, "tensor"),
        P("pipe", None, None, "tensor"),
        P("dp", "tensor"),
        P("dp"),
        P(),
    )
    return jax.shard_map(
        make_local(mesh.shape["pipe"], mesh.shape["dp"], mesh.shape["tensor"]),
        mesh=mesh,
        in_specs=placed,
        out_specs=(
            P("pipe", "dp", "tensor"),
            P("pipe", "dp", "tensor"),
            P("pipe", "dp", None, "tensor"),
            P("pipe", "dp", None, "tensor"),
        ),
        check_vma=False,
    )
```

time: 1630 us -> 885 us (0.54)
  waiting for transfers between devices: 623 us -> 76.6 us
  starting transfers between devices: 76.1 us -> 355 us
  blocking collectives: 268 us -> 13.9 us
  local copies, waits for them, and re-layouts: 284 us -> 95.1 us
  between operations: 42.2 us -> 3.84 us
    ppermute x12 -> x86, starting transfers between devices: 15.9 us -> 355 us  [send(): return lax.ppermute(value, axes, pairs)]
    unnamed x18 -> x0, waiting for transfers between devices: 196 us -> none
    all_gather x14 -> x0, blocking collectives: 163 us -> none  [the longest x7 118 us: local(): lax.all_gather(normed_input, 'dp', axis=0, tiled=True)]
    reduce_scatter x7 -> x0, waiting for transfers between devices: 163 us -> none  [local(): lax.psum_scatter(back_rows(jnp.int32(0), row_count * lax.axis_size('dp'))...]
    psum x7 -> x0, waiting for transfers between devices: 162 us -> none  [local(): lax.psum(wide_parts.astype(jnp.bfloat16), 'tensor').astype(jnp.float32)]
    dynamic_update_slice x21 -> x0, local copies, waits for them, and re-layouts: 127 us -> none  [put_block(): lax.dynamic_update_index_in_dim(buffer, jnp.where(active, value, previous...]
    psum x21 -> x0, blocking collectives: 105 us -> none  [the longest x7 35.3 us: local(): total_sq = lax.psum(squares, 'tensor')]
    all_to_all x14 -> x0, waiting for transfers between devices: 100 us -> none  [the longest x7 54.7 us: local(): lax.all_to_all(partial_value, 'dp', split_axis=0, concat_axis=1, tiled=True)]
  transfers between devices with their start and end apart: 42 -> 86, of which waited for: 30 -> 8; matrix products, arithmetic and copies ran while one was open for 15% -> 46% of each run, Pallas kernels for 0% -> 0%
where the time goes in v1:
time: 885 us; the launch traced here: 874 us
  starting transfers between devices  355 us (40%)
  matrix products  288 us (33%)
  local copies, waits for them, and re-layouts  95.1 us (11%)
  waiting for transfers between devices  76.6 us (9%)
  other arithmetic  41.7 us (5%)
  blocking collectives  13.9 us (2%)
    ppermute x86, starting transfers between devices, send(): return lax.ppermute(value, axes, pairs)  355 us
    dot_general x4, matrix products, local(): lax.dot_general(incoming, w_flat, (((1,), (1,)), ((), ())), preferred_ele...  116 us
    dot_general x4, matrix products, local(): product = jnp.dot(scaled, w_flat, preferred_element_type=F32).astype(BF16)  95.5 us
    ppermute x86, waiting for transfers between devices, send(): return lax.ppermute(value, axes, pairs)  76.6 us
    unnamed x94, local copies, waits for them, and re-layouts  53 us
    dot_general x4, matrix products, local(): lax.dot_general(scaled, down_flat, (((1,), (1,)), ((), ())), preferred_el...  26.5 us
  transfers between devices with their start and end apart: 86, of which 8 were waited for; matrix products, arithmetic and copies ran while one was open for 46% of the time, Pallas kernels for 0%

profile of v1, /device:TPU:0, one launch (start us, length us, event | category | flops | bytes accessed | tf_op | source)
XLA Modules:
  0.0 873.6 jit_solution(8815600668959317435)
XLA Ops:
  18.1 13.9 %all-reduce = s32[16]{0:T(128)S(1)} all-reduce(s32[16]{0:T(128)S(1)} %dynamic-update-slice), channel_id=1, replica_groups=mesh['pipe'=4,'dp'=4,'tensor'=2] {'dp'}, use_global_device_ids=true, to_apply=%add | all-reduce | flops 16 | bytes 128
  33.0 44.4 %copy.88 = bf16[1024,8,2,2048]{3,1,2,0:T(8,128)(2,1)} copy(bf16[1024,8,2,2048]{3,2,1,0:T(2,128)(2,1)} %bitcast.168) | data formatting | bytes 134217728
  88.1 23.8 %convolution_convert_fusion.7 = bf16[128,4096]{1,0:T(8,128)(2,1)} fusion(bf16[8192,4096]{1,0:T(8,128)(2,1)} %bitcast.169, bf16[128,8192]{1,0:T(8,128)(2,1)S(1)} %get-tuple-element.19, f32[8192]{0:T(1024)S(1)} %bitcast.319), kind=kOutput, calls=%fused_computation.17 | convolution fusion | flops 8593604608 | bytes 70287360 | tf_op jit(solution)/shard_map/dot_general | solution.py:130
  161.3 22.8 %convolution_convert_fusion.6 = bf16[128,4096]{1,0:T(8,128)(2,1)S(1)} fusion(bf16[8192,4096]{1,0:T(8,128)(2,1)} %bitcast.169, bf16[128,8192]{1,0:T(8,128)(2,1)S(1)} %get-tuple-element.17, f32[8192]{0:T(1024)S(1)} %bitcast.321), kind=kOutput, calls=%fused_computation.16 | convolution fusion | flops 8593604608 | bytes 70287360 | tf_op jit(solution)/shard_map/dot_general | solution.py:130
  200.3 15.6 %collective-permute-start.16 = (bf16[128,2048]{1,0:T(8,128)(2,1)S(1)}, bf16[128,2048]{1,0:T(8,128)(2,1)S(1)}, u32[]{:S(2)}, u32[]{:S(2)}) collective-permute-start(bf16[128,2048]{1,0:T(8,128)(2,1)S(1)} %get-tuple-element.100), channel_id=1, source_target_pairs={{8,22},{9,23},{10,16},{11,17},{12,18},{13,19},{14,20},{15,21}} | collective-permute-start | bytes 1572872 | tf_op jit(solution)/shard_map/ppermute | solution.py:27
  227.4 26.0 %collective-permute-start.18 = (f32[1,128]{1,0:T(1,128)S(1)}, f32[1,128]{1,0:T(1,128)S(1)}, u32[]{:S(2)}, u32[]{:S(2)}) collective-permute-start(f32[1,128]{1,0:T(1,128)S(1)} %bitcast.404), channel_id=1, source_target_pairs={{16,17},{17,16},{18,19},{19,18},{20,21},{21,20},{22,23},{23,22}} | collective-permute-start | bytes 1544 | tf_op jit(solution)/shard_map/ppermute | solution.py:27
  253.4 24.4 %convolution_convert_fusion.5 = bf16[128,4096]{1,0:T(8,128)(2,1)S(1)} fusion(bf16[8192,4096]{1,0:T(8,128)(2,1)} %bitcast.169, bf16[128,8192]{1,0:T(8,128)(2,1)} %get-tuple-element.15, f32[8192]{0:T(1024)S(1)} %bitcast.323), kind=kOutput, calls=%fused_computation.15 | convolution fusion | flops 8593604608 | bytes 70287360 | tf_op jit(solution)/shard_map/dot_general | solution.py:130
  282.9 6.9 fusion.44
  290.0 8.0 collective-permute-start.19
  302.0 8.9 %collective-permute-start.23 = (bf16[128,2048]{1,0:T(8,128)(2,1)S(1)}, bf16[128,2048]{1,0:T(8,128)(2,1)S(1)}, u32[]{:S(2)}, u32[]{:S(2)}) collective-permute-start(bf16[128,2048]{1,0:T(8,128)(2,1)S(1)} %get-tuple-element.102), channel_id=1, source_target_pairs={{16,30},{17,31},{18,24},{19,25},{20,26},{21,27},{22,28},{23,29}} | collective-permute-start | bytes 1572872 | tf_op jit(solution)/shard_map/ppermute | solution.py:27
  310.9 7.0 collective-permute-start.22
  318.0 7.0 collective-permute-start.21
  331.2 24.4 %convolution_convert_fusion.4 = bf16[128,4096]{1,0:T(8,128)(2,1)S(1)} fusion(bf16[8192,4096]{1,0:T(8,128)(2,1)} %bitcast.169, bf16[128,8192]{1,0:T(8,128)(2,1)} %get-tuple-element.13, f32[8192]{0:T(1024)S(1)} %bitcast.325), kind=kOutput, calls=%fused_computation.14 | convolution fusion | flops 8593604608 | bytes 70287360 | tf_op jit(solution)/shard_map/dot_general | solution.py:130
  360.7 6.9 fusion.47
  367.8 18.5 %collective-permute-start.26 = (f32[16,128]{1,0:T(8,128)S(1)}, f32[16,128]{1,0:T(8,128)S(1)}, u32[]{:S(2)}, u32[]{:S(2)}) collective-permute-start(f32[16,128]{1,0:T(8,128)S(1)} %bitcast.386), channel_id=1, source_target_pairs={{24,25},{25,24},{26,27},{27,26},{28,29},{29,28},{30,31},{31,30}} | collective-permute-start | bytes 24584 | tf_op jit(solution)/shard_map/ppermute | solution.py:27
  401.7 16.2 %collective-permute-start.41 = (f32[17,128]{1,0:T(8,128)S(1)}, f32[17,128]{1,0:T(8,128)S(1)}, u32[]{:S(2)}, u32[]{:S(2)}) collective-permute-start(f32[17,128]{1,0:T(8,128)S(1)} %fusion.190), channel_id=1, source_target_pairs={{24,26},{25,27},{26,28},{27,29},{28,30},{29,31},{30,24},{31,25}} | collective-permute-start | bytes 26120 | tf_op jit(solution)/shard_map/ppermute | solution.py:27
  420.6 29.1 %convolution_convert_fusion.3 = bf16[128,8192]{1,0:T(8,128)(2,1)} fusion(bf16[8192,4096]{1,0:T(8,128)(2,1)} %bitcast.169, bf16[128,2048]{1,0:T(8,128)(2,1)} %get-tuple-element.73, bf16[128,2048]{1,0:T(8,128)(2,1)} %get-tuple-element.72), kind=kOutput, calls=%fused_computation.5 | convolution fusion | flops 8593080320 | bytes 70254592 | tf_op jit(solution)/shard_map/dot_general | solution.py:168
  466.8 35.4 %collective-permute-start.44 = (bf16[128,2048]{1,0:T(8,128)(2,1)}, bf16[128,2048]{1,0:T(8,128)(2,1)S(1)}, u32[]{:S(2)}, u32[]{:S(2)}) collective-permute-start(bf16[128,2048]{1,0:T(8,128)(2,1)} %get-tuple-element.41), channel_id=1, source_target_pairs={{24,16},{25,17},{26,18},{27,19},{28,20},{29,21},{30,22},{31,23}} | collective-permute-start | bytes 1572872 | tf_op jit(solution)/shard_map/ppermute | solution.py:27
  503.9 8.7 collective-permute-start.30
  512.6 7.6 collective-permute-start.49
  529.0 29.0 %convolution_convert_fusion.2 = bf16[128,8192]{1,0:T(8,128)(2,1)} fusion(bf16[8192,4096]{1,0:T(8,128)(2,1)} %bitcast.169, bf16[128,2048]{1,0:T(8,128)(2,1)} %get-tuple-element.71, bf16[128,2048]{1,0:T(8,128)(2,1)S(1)} %get-tuple-element.70), kind=kOutput, calls=%fused_computation.4 | convolution fusion | flops 8593080320 | bytes 70254592 | tf_op jit(solution)/shard_map/dot_general | solution.py:168
  563.4 13.7 %collective-permute-start.54 = (f32[17,128]{1,0:T(8,128)S(1)}, f32[17,128]{1,0:T(8,128)S(1)}, u32[]{:S(2)}, u32[]{:S(2)}) collective-permute-start(f32[17,128]{1,0:T(8,128)S(1)} %fusion.189), channel_id=1, source_target_pairs={{16,18},{17,19},{18,20},{19,21},{20,22},{21,23},{22,16},{23,17}} | collective-permute-start | bytes 26120 | tf_op jit(solution)/shard_map/ppermute | solution.py:27
  579.2 8.0 collective-permute-start.52
  587.2 7.0 collective-permute-start.51
  602.2 27.7 %collective-permute-start.62 = (bf16[128,2048]{1,0:T(8,128)(2,1)}, bf16[128,2048]{1,0:T(8,128)(2,1)}, u32[]{:S(2)}, u32[]{:S(2)}) collective-permute-start(bf16[128,2048]{1,0:T(8,128)(2,1)} %fusion.58), channel_id=1, source_target_pairs={{16,9},{17,8},{18,11},{19,10},{20,13},{21,12},{22,15},{23,14}} | collective-permute-start | bytes 1572872 | tf_op jit(solution)/shard_map/ppermute | solution.py:27
  641.4 29.0 %convolution_convert_fusion.1 = bf16[128,8192]{1,0:T(8,128)(2,1)} fusion(bf16[8192,4096]{1,0:T(8,128)(2,1)} %bitcast.169, bf16[128,2048]{1,0:T(8,128)(2,1)} %get-tuple-element.69, bf16[128,2048]{1,0:T(8,128)(2,1)S(1)} %get-tuple-element.68), kind=kOutput, calls=%fused_computation.3 | convolution fusion | flops 8593080320 | bytes 70254592 | tf_op jit(solution)/shard_map/dot_general | solution.py:168
  698.3 44.1 %collective-permute-done.70 = bf16[128,2048]{1,0:T(8,128)(2,1)S(1)} collective-permute-done((bf16[128,2048]{1,0:T(8,128)(2,1)}, bf16[128,2048]{1,0:T(8,128)(2,1)S(1)}, u32[]{:S(2)}, u32[]{:S(2)}) %collective-permute-start.70) | collective-permute-done | bytes 524320 | tf_op jit(solution)/shard_map/ppermute | solution.py:27
  752.0 29.0 %convolution_convert_fusion = bf16[128,8192]{1,0:T(8,128)(2,1)} fusion(bf16[8192,4096]{1,0:T(8,128)(2,1)} %bitcast.169, bf16[128,2048]{1,0:T(8,128)(2,1)} %get-tuple-element.67, bf16[128,2048]{1,0:T(8,128)(2,1)S(1)} %get-tuple-element.66), kind=kOutput, calls=%fused_computation.2 | convolution fusion | flops 8593080320 | bytes 70254592 | tf_op jit(solution)/shard_map/dot_general | solution.py:168
  810.3 15.8 %collective-permute-start.76 = (bf16[128,2048]{1,0:T(8,128)(2,1)S(1)}, bf16[128,2048]{1,0:T(8,128)(2,1)S(1)}, u32[]{:S(2)}, u32[]{:S(2)}) collective-permute-start(bf16[128,2048]{1,0:T(8,128)(2,1)S(1)} %copy-done.28), channel_id=1, source_target_pairs={{0,2},{1,3},{2,4},{3,5},{4,6},{5,7},{6,0},{7,1}} | collective-permute-start | bytes 1572872 | tf_op jit(solution)/shard_map/ppermute | solution.py:27
  835.0 6.8 collective-permute-done.78
  841.8 7.2 collective-permute-done.77
  851.9 6.9 collective-permute-start.85
  (391 shorter events, 289.9 us)
Async XLA Ops:
  0.6 76.8 %collective-permute-start = (bf16[32,8192]{1,0:T(8,128)(2,1)}, bf16[32,8192]{1,0:T(8,128)(2,1)S(1)}, u32[]{:S(2)}, u32[]{:S(2)}) collective-permute-start(bf16[32,8192]{1,0:T(8,128)(2,1)} %param.8), channel_id=1, source_target_pairs={{0,2},{1,3},{2,4},{3,5},{4,6},{5,7},{6,0},{7,1}} | collective-permute-start | bytes 1572872 | tf_op jit(solution)/shard_map/ppermute | solution.py:27
  5.6 72.6 %collective-permute-start.2 = (bf16[32,8192]{1,0:T(8,128)(2,1)}, bf16[32,8192]{1,0:T(8,128)(2,1)S(1)}, u32[]{:S(2)}, u32[]{:S(2)}) collective-permute-start(bf16[32,8192]{1,0:T(8,128)(2,1)} %param.8), channel_id=1, source_target_pairs={{0,6},{1,7},{2,0},{3,1},{4,2},{5,3},{6,4},{7,5}} | collective-permute-start | bytes 1572872 | tf_op jit(solution)/shard_map/ppermute | solution.py:27
  9.5 68.6 %collective-permute-start.1 = (bf16[32,8192]{1,0:T(8,128)(2,1)}, bf16[32,8192]{1,0:T(8,128)(2,1)S(1)}, u32[]{:S(2)}, u32[]{:S(2)}) collective-permute-start(bf16[32,8192]{1,0:T(8,128)(2,1)} %param.8), channel_id=1, source_target_pairs={{0,4},{1,5},{2,6},{3,7},{4,0},{5,1},{6,2},{7,3}} | collective-permute-start | bytes 1572872 | tf_op jit(solution)/shard_map/ppermute | solution.py:27
  12.4 68.3 %collective-permute-start.33 = (bf16[32,8192]{1,0:T(8,128)(2,1)}, bf16[32,8192]{1,0:T(8,128)(2,1)}, u32[]{:S(2)}, u32[]{:S(2)}) collective-permute-start(bf16[32,8192]{1,0:T(8,128)(2,1)} %param.13), channel_id=1, source_target_pairs={{24,26},{25,27},{26,28},{27,29},{28,30},{29,31},{30,24},{31,25}} | collective-permute-start | bytes 1572872 | tf_op jit(solution)/shard_map/ppermute | solution.py:27
  13.9 66.8 %collective-permute-start.35 = (bf16[32,8192]{1,0:T(8,128)(2,1)}, bf16[32,8192]{1,0:T(8,128)(2,1)}, u32[]{:S(2)}, u32[]{:S(2)}) collective-permute-start(bf16[32,8192]{1,0:T(8,128)(2,1)} %param.13), channel_id=1, source_target_pairs={{24,30},{25,31},{26,24},{27,25},{28,26},{29,27},{30,28},{31,29}} | collective-permute-start | bytes 1572872 | tf_op jit(solution)/shard_map/ppermute | solution.py:27
  84.5 47.7 %collective-permute-start.4 = (f32[1,128]{1,0:T(1,128)S(1)}, f32[1,128]{1,0:T(1,128)S(1)}, u32[]{:S(2)}, u32[]{:S(2)}) collective-permute-start(f32[1,128]{1,0:T(1,128)S(1)} %bitcast.405), channel_id=1, source_target_pairs={{0,1},{1,0},{2,3},{3,2},{4,5},{5,4},{6,7},{7,6}} | collective-permute-start | bytes 1544 | tf_op jit(solution)/shard_map/ppermute | solution.py:27
  160.6 35.9 %collective-permute-start.11 = (f32[1,128]{1,0:T(1,128)S(1)}, f32[1,128]{1,0:T(1,128)S(1)}, u32[]{:S(2)}, u32[]{:S(2)}) collective-permute-start(f32[1,128]{1,0:T(1,128)S(1)} %bitcast.403), channel_id=1, source_target_pairs={{8,9},{9,8},{10,11},{11,10},{12,13},{13,12},{14,15},{15,14}} | collective-permute-start | bytes 1544 | tf_op jit(solution)/shard_map/ppermute | solution.py:27
  227.4 70.9 %collective-permute-start.18 = (f32[1,128]{1,0:T(1,128)S(1)}, f32[1,128]{1,0:T(1,128)S(1)}, u32[]{:S(2)}, u32[]{:S(2)}) collective-permute-start(f32[1,128]{1,0:T(1,128)S(1)} %bitcast.404), channel_id=1, source_target_pairs={{16,17},{17,16},{18,19},{19,18},{20,21},{21,20},{22,23},{23,22}} | collective-permute-start | bytes 1544 | tf_op jit(solution)/shard_map/ppermute | solution.py:27
  326.6 236.1 %collective-permute-start.32 = (bf16[32,8192]{1,0:T(8,128)(2,1)}, bf16[32,8192]{1,0:T(8,128)(2,1)}, u32[]{:S(2)}, u32[]{:S(2)}) collective-permute-start(bf16[32,8192]{1,0:T(8,128)(2,1)} %constant_dynamic-slice_fusion.22), channel_id=1, source_target_pairs={{8,0},{9,1},{10,2},{11,3},{12,4},{13,5},{14,6},{15,7}} | collective-permute-start | bytes 1572872 | tf_op jit(solution)/shard_map/ppermute | solution.py:27
  330.1 57.2 %collective-permute-start.25 = (f32[1,128]{1,0:T(1,128)S(1)}, f32[1,128]{1,0:T(1,128)S(1)}, u32[]{:S(2)}, u32[]{:S(2)}) collective-permute-start(f32[1,128]{1,0:T(1,128)S(1)} %bitcast.402), channel_id=1, source_target_pairs={{24,25},{25,24},{26,27},{27,26},{28,29},{29,28},{30,31},{31,30}} | collective-permute-start | bytes 1544 | tf_op jit(solution)/shard_map/ppermute | solution.py:27
  400.4 53.7 %collective-permute-start.43 = (f32[17,128]{1,0:T(8,128)S(1)}, f32[17,128]{1,0:T(8,128)S(1)}, u32[]{:S(2)}, u32[]{:S(2)}) collective-permute-start(f32[17,128]{1,0:T(8,128)S(1)} %fusion.190), channel_id=1, source_target_pairs={{24,30},{25,31},{26,24},{27,25},{28,26},{29,27},{30,28},{31,29}} | collective-permute-start | bytes 26120 | tf_op jit(solution)/shard_map/ppermute | solution.py:27
  401.1 54.5 %collective-permute-start.42 = (f32[17,128]{1,0:T(8,128)S(1)}, f32[17,128]{1,0:T(8,128)S(1)}, u32[]{:S(2)}, u32[]{:S(2)}) collective-permute-start(f32[17,128]{1,0:T(8,128)S(1)} %fusion.190), channel_id=1, source_target_pairs={{24,28},{25,29},{26,30},{27,31},{28,24},{29,25},{30,26},{31,27}} | collective-permute-start | bytes 26120 | tf_op jit(solution)/shard_map/ppermute | solution.py:27
  401.7 55.3 %collective-permute-start.41 = (f32[17,128]{1,0:T(8,128)S(1)}, f32[17,128]{1,0:T(8,128)S(1)}, u32[]{:S(2)}, u32[]{:S(2)}) collective-permute-start(f32[17,128]{1,0:T(8,128)S(1)} %fusion.190), channel_id=1, source_target_pairs={{24,26},{25,27},{26,28},{27,29},{28,30},{29,31},{30,24},{31,25}} | collective-permute-start | bytes 26120 | tf_op jit(solution)/shard_map/ppermute | solution.py:27
  462.2 40.1 %collective-permute-start.29 = (bf16[32,2048]{1,0:T(8,128)(2,1)}, bf16[32,2048]{1,0:T(8,128)(2,1)S(1)}, u32[]{:S(2)}, u32[]{:S(2)}) collective-permute-start(bf16[32,2048]{1,0:T(8,128)(2,1)} %get-tuple-element.95), channel_id=1, source_target_pairs={{24,30},{25,31},{26,24},{27,25},{28,26},{29,27},{30,28},{31,29}} | collective-permute-start | bytes 393224 | tf_op jit(solution)/shard_map/ppermute | solution.py:27
  462.9 41.0 %collective-permute-start.28 = (bf16[32,2048]{1,0:T(8,128)(2,1)}, bf16[32,2048]{1,0:T(8,128)(2,1)S(1)}, u32[]{:S(2)}, u32[]{:S(2)}) collective-permute-start(bf16[32,2048]{1,0:T(8,128)(2,1)} %get-tuple-element.96), channel_id=1, source_target_pairs={{24,28},{25,29},{26,30},{27,31},{28,24},{29,25},{30,26},{31,27}} | collective-permute-start | bytes 393224 | tf_op jit(solution)/shard_map/ppermute | solution.py:27
  463.6 49.0 %collective-permute-start.27 = (bf16[32,2048]{1,0:T(8,128)(2,1)S(1)}, bf16[32,2048]{1,0:T(8,128)(2,1)}, u32[]{:S(2)}, u32[]{:S(2)}) collective-permute-start(bf16[32,2048]{1,0:T(8,128)(2,1)S(1)} %get-tuple-element.97), channel_id=1, source_target_pairs={{24,26},{25,27},{26,28},{27,29},{28,30},{29,31},{30,24},{31,25}} | collective-permute-start | bytes 393224 | tf_op jit(solution)/shard_map/ppermute | solution.py:27
  466.8 55.2 %collective-permute-start.44 = (bf16[128,2048]{1,0:T(8,128)(2,1)}, bf16[128,2048]{1,0:T(8,128)(2,1)S(1)}, u32[]{:S(2)}, u32[]{:S(2)}) collective-permute-start(bf16[128,2048]{1,0:T(8,128)(2,1)} %get-tuple-element.41), channel_id=1, source_target_pairs={{24,16},{25,17},{26,18},{27,19},{28,20},{29,21},{30,22},{31,23}} | collective-permute-start | bytes 1572872 | tf_op jit(solution)/shard_map/ppermute | solution.py:27
  502.4 61.0 %collective-permute-start.31 = (bf16[32,8192]{1,0:T(8,128)(2,1)}, bf16[32,8192]{1,0:T(8,128)(2,1)}, u32[]{:S(2)}, u32[]{:S(2)}) collective-permute-start(bf16[32,8192]{1,0:T(8,128)(2,1)} %constant_dynamic-slice_fusion.23), channel_id=1, source_target_pairs={{16,8},{17,9},{18,10},{19,11},{20,12},{21,13},{22,14},{23,15}} | collective-permute-start | bytes 1572872 | tf_op jit(solution)/shard_map/ppermute | solution.py:27
  503.9 73.2 %collective-permute-start.30 = (bf16[32,8192]{1,0:T(8,128)(2,1)}, bf16[32,8192]{1,0:T(8,128)(2,1)}, u32[]{:S(2)}, u32[]{:S(2)}) collective-permute-start(bf16[32,8192]{1,0:T(8,128)(2,1)} %constant_dynamic-slice_fusion.24), channel_id=1, source_target_pairs={{24,16},{25,17},{26,18},{27,19},{28,20},{29,21},{30,22},{31,23}} | collective-permute-start | bytes 1572872 | tf_op jit(solution)/shard_map/ppermute | solution.py:27
  526.1 35.9 %collective-permute-start.53 = (f32[17,128]{1,0:T(8,128)S(1)}, f32[17,128]{1,0:T(8,128)S(1)}, u32[]{:S(2)}, u32[]{:S(2)}) collective-permute-start(f32[17,128]{1,0:T(8,128)S(1)} %pad_maximum_fusion.19), channel_id=1, source_target_pairs={{16,17},{17,16},{18,19},{19,18},{20,21},{21,20},{22,23},{23,22}} | collective-permute-start | bytes 26120 | tf_op jit(solution)/shard_map/ppermute | solution.py:27
  560.5 36.8 %collective-permute-start.50 = (bf16[128,2048]{1,0:T(8,128)(2,1)}, bf16[128,2048]{1,0:T(8,128)(2,1)}, u32[]{:S(2)}, u32[]{:S(2)}) collective-permute-start(bf16[128,2048]{1,0:T(8,128)(2,1)} %get-tuple-element.34), channel_id=1, source_target_pairs={{16,18},{17,19},{18,20},{19,21},{20,22},{21,23},{22,16},{23,17}} | collective-permute-start | bytes 1572872 | tf_op jit(solution)/shard_map/ppermute | solution.py:27
  563.4 32.3 %collective-permute-start.54 = (f32[17,128]{1,0:T(8,128)S(1)}, f32[17,128]{1,0:T(8,128)S(1)}, u32[]{:S(2)}, u32[]{:S(2)}) collective-permute-start(f32[17,128]{1,0:T(8,128)S(1)} %fusion.189), channel_id=1, source_target_pairs={{16,18},{17,19},{18,20},{19,21},{20,22},{21,23},{22,16},{23,17}} | collective-permute-start | bytes 26120 | tf_op jit(solution)/shard_map/ppermute | solution.py:27
  594.2 36.4 %collective-permute-start.47 = (bf16[128,2048]{1,0:T(8,128)(2,1)S(1)}, bf16[128,2048]{1,0:T(8,128)(2,1)}, u32[]{:S(2)}, u32[]{:S(2)}) collective-permute-start(bf16[128,2048]{1,0:T(8,128)(2,1)S(1)} %collective-permute-done.44), channel_id=1, source_target_pairs={{16,22},{17,23},{18,16},{19,17},{20,18},{21,19},{22,20},{23,21}} | collective-permute-start | bytes 1572872 | tf_op jit(solution)/shard_map/ppermute | solution.py:27
  595.7 34.9 %collective-permute-start.46 = (bf16[128,2048]{1,0:T(8,128)(2,1)S(1)}, bf16[128,2048]{1,0:T(8,128)(2,1)}, u32[]{:S(2)}, u32[]{:S(2)}) collective-permute-start(bf16[128,2048]{1,0:T(8,128)(2,1)S(1)} %collective-permute-done.44), channel_id=1, source_target_pairs={{16,20},{17,21},{18,22},{19,23},{20,16},{21,17},{22,18},{23,19}} | collective-permute-start | bytes 1572872 | tf_op jit(solution)/shard_map/ppermute | solution.py:27
  597.3 33.3 %collective-permute-start.45 = (bf16[128,2048]{1,0:T(8,128)(2,1)S(1)}, bf16[128,2048]{1,0:T(8,128)(2,1)S(1)}, u32[]{:S(2)}, u32[]{:S(2)}) collective-permute-start(bf16[128,2048]{1,0:T(8,128)(2,1)S(1)} %collective-permute-done.44), channel_id=1, source_target_pairs={{16,18},{17,19},{18,20},{19,21},{20,22},{21,23},{22,16},{23,17}} | collective-permute-start | bytes 1572872 | tf_op jit(solution)/shard_map/ppermute | solution.py:27
  602.2 36.9 %collective-permute-start.62 = (bf16[128,2048]{1,0:T(8,128)(2,1)}, bf16[128,2048]{1,0:T(8,128)(2,1)}, u32[]{:S(2)}, u32[]{:S(2)}) collective-permute-start(bf16[128,2048]{1,0:T(8,128)(2,1)} %fusion.58), channel_id=1, source_target_pairs={{16,9},{17,8},{18,11},{19,10},{20,13},{21,12},{22,15},{23,14}} | collective-permute-start | bytes 1572872 | tf_op jit(solution)/shard_map/ppermute | solution.py:27
  638.2 36.1 %collective-permute-start.66 = (f32[17,128]{1,0:T(8,128)S(1)}, f32[17,128]{1,0:T(8,128)S(1)}, u32[]{:S(2)}, u32[]{:S(2)}) collective-permute-start(f32[17,128]{1,0:T(8,128)S(1)} %pad_maximum_fusion.20), channel_id=1, source_target_pairs={{8,9},{9,8},{10,11},{11,10},{12,13},{13,12},{14,15},{15,14}} | collective-permute-start | bytes 26120 | tf_op jit(solution)/shard_map/ppermute | solution.py:27
  685.0 187.1 %collective-permute-start.48 = (bf16[32,8192]{1,0:T(8,128)(2,1)}, bf16[32,8192]{1,0:T(8,128)(2,1)}, u32[]{:S(2)}, u32[]{:S(2)}) collective-permute-start(bf16[32,8192]{1,0:T(8,128)(2,1)} %constant_dynamic-slice_fusion.16), channel_id=1, source_target_pairs={{16,24},{17,25},{18,26},{19,27},{20,28},{21,29},{22,30},{23,31}} | collective-permute-start | bytes 1572872 | tf_op jit(solution)/shard_map/ppermute | solution.py:27
  690.4 59.3 %collective-permute-start.75 = (bf16[128,2048]{1,0:T(8,128)(2,1)}, bf16[128,2048]{1,0:T(8,128)(2,1)}, u32[]{:S(2)}, u32[]{:S(2)}) collective-permute-start(bf16[128,2048]{1,0:T(8,128)(2,1)} %fusion.55), channel_id=1, source_target_pairs={{8,1},{9,0},{10,3},{11,2},{12,5},{13,4},{14,7},{15,6}} | collective-permute-start | bytes 1572872 | tf_op jit(solution)/shard_map/ppermute | solution.py:27
  691.7 50.6 %collective-permute-start.70 = (bf16[128,2048]{1,0:T(8,128)(2,1)}, bf16[128,2048]{1,0:T(8,128)(2,1)S(1)}, u32[]{:S(2)}, u32[]{:S(2)}) collective-permute-start(bf16[128,2048]{1,0:T(8,128)(2,1)} %fusion.55), channel_id=1, source_target_pairs={{8,0},{9,1},{10,2},{11,3},{12,4},{13,5},{14,6},{15,7}} | collective-permute-start | bytes 1572872 | tf_op jit(solution)/shard_map/ppermute | solution.py:27
  696.8 175.3 %collective-permute-start.61 = (bf16[32,8192]{1,0:T(8,128)(2,1)}, bf16[32,8192]{1,0:T(8,128)(2,1)}, u32[]{:S(2)}, u32[]{:S(2)}) collective-permute-start(bf16[32,8192]{1,0:T(8,128)(2,1)} %constant_dynamic-slice_fusion.12), channel_id=1, source_target_pairs={{8,16},{9,17},{10,18},{11,19},{12,20},{13,21},{14,22},{15,23}} | collective-permute-start | bytes 1572872 | tf_op jit(solution)/shard_map/ppermute | solution.py:27
  746.4 34.6 %collective-permute-start.79 = (f32[17,128]{1,0:T(8,128)S(1)}, f32[17,128]{1,0:T(8,128)S(1)}, u32[]{:S(2)}, u32[]{:S(2)}) collective-permute-start(f32[17,128]{1,0:T(8,128)S(1)} %pad_maximum_fusion.21), channel_id=1, source_target_pairs={{0,1},{1,0},{2,3},{3,2},{4,5},{5,4},{6,7},{7,6}} | collective-permute-start | bytes 26120 | tf_op jit(solution)/shard_map/ppermute | solution.py:27
  (96 other events, 1154.5 us)

commit v2 on v1

--- a/solution.py
+++ b/solution.py
@@ -44,13 +44,25 @@
         up_flat = resident_up[0].reshape(slots * rank, width_local)
         first_col = dp_id * piece_cols
 
+        def gather_dp(parts_by_shift, axis):
+            stacked = jnp.stack(parts_by_shift)
+            order = [
+                lax.dynamic_index_in_dim(stacked, (dp_id - d) % dp_count, 0, keepdims=False)
+                for d in range(dp_count)
+            ]
+            return jnp.concatenate(order, axis=axis)
+
         def own_cols(array):
             return lax.dynamic_slice_in_dim(array, first_col, piece_cols, array.ndim - 1)
 
         down_cols = own_cols(down_flat)
         up_cols = own_cols(up_flat)
         gain_cols = own_cols(gain_row)
-        all_tenants = lax.all_gather(batch_tenants, "dp", axis=0, tiled=True)
+        tenant_parts = [batch_tenants] + [
+            lax.ppermute(batch_tenants, "dp", [(d, (d + s) % dp_count) for d in range(dp_count)])
+            for s in range(1, dp_count)
+        ]
+        all_tenants = gather_dp(tenant_parts, 0)
         labels = jnp.arange(slots, dtype=jnp.int32)
         slot_ids = jnp.sum(
             jnp.where(all_tenants[:, None] == labels[None, :], tenant_slots[None, :], 0), axis=1
@@ -71,14 +83,6 @@
             wide = jnp.tile(values, (1, slots))
             return jnp.where(lane_pick, wide, jnp.zeros((), values.dtype))
 
-        def gather_dp(parts_by_shift, axis):
-            stacked = jnp.stack(parts_by_shift)
-            order = [
-                lax.dynamic_index_in_dim(stacked, (dp_id - d) % dp_count, 0, keepdims=False)
-                for d in range(dp_count)
-            ]
-            return jnp.concatenate(order, axis=axis)
-
         def gather_tensor(parts_by_shift):
             stacked = jnp.stack(parts_by_shift)
             order = [
@@ -123,11 +127,21 @@
             wide = state.astype(F32)
             squares = sum_tensor(jnp.sum(wide * wide, axis=1)[None, :], k)
             scaled = (wide * gain_row[None, :]).astype(BF16)
-            low_part = narrow(
-                lax.dot_general(scaled, down_flat, (((1,), (1,)), ((), ())), preferred_element_type=F32)
-            )
-            low_raw = sum_tensor(low_part, k)
-            product = jnp.dot(scaled, w_flat, preferred_element_type=F32).astype(BF16)
+
+            def project(values):
+                low = lax.dot_general(
+                    values, down_flat, (((1,), (1,)), ((), ())), preferred_element_type=F32
+                )
+                return jnp.dot(values, w_flat, preferred_element_type=F32).astype(BF16), low
+
+            def skipped(values):
+                return (
+                    jnp.zeros((rows, tensor_count * piece_cols), BF16),
+                    jnp.zeros((rows, slots * rank), F32),
+                )
+
+            product, all_terms = lax.cond(section_id == k, project, skipped, scaled)
+            low_raw = sum_tensor(narrow(all_terms), k)
             blocks = product.reshape(rows, tensor_count, piece_cols)
             base = jnp.zeros((rows, piece_cols), F32)
             for shift in range(tensor_count):
@@ -165,9 +179,21 @@
             stat_part = jnp.sum(grad_wide * branch, axis=1)
             small = sum_dp(sum_tensor(jnp.concatenate([low_part, stat_part[None, :]], axis=0), k), k)
             incoming = gather_tensor(grad_parts)
-            partial = lax.dot_general(
-                incoming, w_flat, (((1,), (1,)), ((), ())), preferred_element_type=F32
-            ).astype(BF16)
+            if k == last:
+                grad_full = cot_full
+            else:
+                grad_full = gather_dp(dp_all(grad_cols, k, k), 1)
+
+            def back(values):
+                return lax.dot_general(
+                    values, w_flat, (((1,), (1,)), ((), ())), preferred_element_type=F32
+                ).astype(BF16)
+
+            def back_skipped(values):
+                return jnp.zeros((rows, width_local), BF16)
+
+            partial = lax.cond(section_id == k, back, back_skipped, incoming)
+            partial, grad_full = lax.optimization_barrier((partial, grad_full))
             frozen = jnp.zeros((rows, piece_cols), F32)
             for shift in range(dp_count):
                 at = ((dp_id + shift) % dp_count) * piece_cols
@@ -175,10 +201,7 @@
                 if shift:
                     block = send(block, k, k, shift)
                 frozen = frozen + block.astype(F32)
-            if k == last:
-                grad_full = cot_full
-            else:
-                grad_full = gather_dp(dp_all(grad_cols, k, k), 1)
+            if k < last:
                 grad_rows[k + 1] = send(own_row_block(grad_full), k, k + 1)
             low_grad = small[:rank].astype(BF16).T
             statistic = small[rank]

time: 885 us -> 860 us (0.972)
  matrix products: 288 us -> 99.3 us
  starting transfers between devices: 355 us -> 490 us
  waiting for transfers between devices: 76.6 us -> 140 us
  blocking collectives: 13.9 us -> 0 us
  local copies, waits for them, and re-layouts: 95.1 us -> 84.2 us
  other arithmetic: 41.7 us -> 31.4 us
    dot_general x12 -> x3, matrix products: 238 us -> 55 us  [the longest x1 29.2 us: back(): lax.dot_general(values, w_flat, (((1,), (1,)), ((), ())), preferred_eleme...]
    ppermute x86, starting transfers between devices: 355 us -> 471 us  [send(): return lax.ppermute(value, axes, pairs)]
    ppermute x86, waiting for transfers between devices: 76.6 us -> 140 us  [send(): return lax.ppermute(value, axes, pairs)]
    ppermute x0 -> x3, starting transfers between devices: none -> 18.6 us  [local(): lax.ppermute(batch_tenants, 'dp', [(d, (d + s) % dp_count) for d in range...]
    unnamed x1 -> x0, blocking collectives: 13.9 us -> none
    dynamic_slice x7 -> x0, local copies, waits for them, and re-layouts: 9.97 us -> none  [local(): lax.dynamic_index_in_dim(blocks, (tensor_id + shift) % tensor_count, 1, k...]
    unnamed x94 -> x85, local copies, waits for them, and re-layouts: 53 us -> 50.9 us
  transfers between devices with their start and end apart: 86 -> 89, of which waited for: 8 -> 14; matrix products, arithmetic and copies ran while one was open for 46% -> 21% of each run, Pallas kernels for 0% -> 0%
where the time goes in v2:
time: 860 us; the launch traced here: 849 us
  starting transfers between devices  490 us (57%)
  waiting for transfers between devices  140 us (16%)
  matrix products  99.3 us (12%)
  local copies, waits for them, and re-layouts  84.2 us (10%)
  other arithmetic  31.4 us (4%)
    ppermute x86, starting transfers between devices, send(): return lax.ppermute(value, axes, pairs)  471 us
    ppermute x86, waiting for transfers between devices, send(): return lax.ppermute(value, axes, pairs)  140 us
    unnamed x85, local copies, waits for them, and re-layouts  50.9 us
    dot_general x1, matrix products, back(): lax.dot_general(values, w_flat, (((1,), (1,)), ((), ())), preferred_eleme...  29.2 us
    dot_general x1, matrix products, project(): jnp.dot(values, w_flat, preferred_element_type=F32).astype(BF16)  22.8 us
    ppermute x3, starting transfers between devices, local(): lax.ppermute(batch_tenants, 'dp', [(d, (d + s) % dp_count) for d in range...  18.6 us
  transfers between devices with their start and end apart: 89, of which 14 were waited for; matrix products, arithmetic and copies ran while one was open for 21% of the time, Pallas kernels for 0%

profile of v2, /device:TPU:0, one launch (start us, length us, event | category | flops | bytes accessed | tf_op | source)
XLA Modules:
  0.0 849.4 jit_solution(7812832077694076807)
XLA Ops:
  0.6 7.1 collective-permute-start.5
  7.8 5.7 collective-permute-start.7
  13.5 5.7 collective-permute-start.6
  27.1 44.3 %copy.92 = bf16[1024,8,2,2048]{3,1,2,0:T(8,128)(2,1)} copy(bf16[1024,8,2,2048]{3,2,1,0:T(2,128)(2,1)} %bitcast.180) | data formatting | bytes 134217728
  79.1 10.1 %collective-permute-done.1 = bf16[32,8192]{1,0:T(8,128)(2,1)S(1)} collective-permute-done((bf16[32,8192]{1,0:T(8,128)(2,1)S(1)}, bf16[32,8192]{1,0:T(8,128)(2,1)S(1)}, u32[]{:S(2)}, u32[]{:S(2)}) %collective-permute-start.1) | collective-permute-done | bytes 524320 | tf_op jit(solution)/shard_map/ppermute | solution.py:27
  97.1 26.8 %conditional.8 = (f32[128,512]{1,0:T(8,128)S(1)}, bf16[128,2,2048]{2,0,1:T(8,128)(2,1)}) conditional(s32[]{:T(128)} %convert_element_type.219, () %tuple.76, (bf16[128,8192]{1,0:T(8,128)(2,1)S(1)}, bf16[512,8192]{1,0:T(8,128)(2,1)S(1)}, bf16[8192,4096]{1,0:T(8,128)(2,1)}) %tuple.188), branch_computations={%region_0.1_spmd, %region_1.2_spmd} | conditional | flops 9664200704 | bytes 83099664 | solution.py:143
  100.1 22.8 %convolution_convert_fusion = bf16[128,4096]{1,0:T(8,128)(2,1)S(1)} fusion(bf16[128,8192]{1,0:T(8,128)(2,1)S(1)} %get-tuple-element.56, bf16[8192,4096]{1,0:T(8,128)(2,1)} %get-tuple-element.58), kind=kOutput, calls=%fused_computation | convolution fusion | flops 8590458880 | bytes 70254592 | tf_op jit(solution)/shard_map/cond/branch_1_fun/dot_general | solution.py:135
  148.1 5.6 collective-permute-done.11
  153.7 5.6 collective-permute-done.10
  171.9 46.5 %collective-permute-start.19 = (bf16[128,2048]{1,0:T(8,128)(2,1)S(1)}, bf16[128,2048]{1,0:T(8,128)(2,1)S(1)}, u32[]{:S(2)}, u32[]{:S(2)}) collective-permute-start(bf16[128,2048]{1,0:T(8,128)(2,1)S(1)} %get-tuple-element.207), channel_id=1, source_target_pairs={{8,22},{9,23},{10,16},{11,17},{12,18},{13,19},{14,20},{15,21}} | collective-permute-start | bytes 1572872 | tf_op jit(solution)/shard_map/ppermute | solution.py:27
  218.5 6.4 collective-permute-start.18
  224.9 6.4 collective-permute-start.17
  233.8 23.1 %collective-permute-start.21 = (f32[1,128]{1,0:T(1,128)S(1)}, f32[1,128]{1,0:T(1,128)S(1)}, u32[]{:S(2)}, u32[]{:S(2)}) collective-permute-start(f32[1,128]{1,0:T(1,128)S(1)} %bitcast.450), channel_id=1, source_target_pairs={{16,17},{17,16},{18,19},{19,18},{20,21},{21,20},{22,23},{23,22}} | collective-permute-start | bytes 1544 | tf_op jit(solution)/shard_map/ppermute | solution.py:27
  261.8 37.4 %collective-permute-start.22 = (f32[16,128]{1,0:T(8,128)S(1)}, f32[16,128]{1,0:T(8,128)S(1)}, u32[]{:S(2)}, u32[]{:S(2)}) collective-permute-start(f32[16,128]{1,0:T(8,128)S(1)} %bitcast.434), channel_id=1, source_target_pairs={{16,17},{17,16},{18,19},{19,18},{20,21},{21,20},{22,23},{23,22}} | collective-permute-start | bytes 24584 | tf_op jit(solution)/shard_map/ppermute | solution.py:27
  302.8 9.2 %collective-permute-start.26 = (bf16[128,2048]{1,0:T(8,128)(2,1)S(1)}, bf16[128,2048]{1,0:T(8,128)(2,1)S(1)}, u32[]{:S(2)}, u32[]{:S(2)}) collective-permute-start(bf16[128,2048]{1,0:T(8,128)(2,1)S(1)} %get-tuple-element.209), channel_id=1, source_target_pairs={{16,30},{17,31},{18,24},{19,25},{20,26},{21,27},{22,28},{23,29}} | collective-permute-start | bytes 1572872 | tf_op jit(solution)/shard_map/ppermute | solution.py:27
  311.9 7.0 collective-permute-start.25
  319.0 7.0 collective-permute-start.24
  336.3 47.4 %collective-permute-start.29 = (f32[16,128]{1,0:T(8,128)S(1)}, f32[16,128]{1,0:T(8,128)S(1)}, u32[]{:S(2)}, u32[]{:S(2)}) collective-permute-start(f32[16,128]{1,0:T(8,128)S(1)} %bitcast.431), channel_id=1, source_target_pairs={{24,25},{25,24},{26,27},{27,26},{28,29},{29,28},{30,31},{31,30}} | collective-permute-start | bytes 24584 | tf_op jit(solution)/shard_map/ppermute | solution.py:27
  412.1 56.5 %collective-permute-start.33 = (bf16[32,8192]{1,0:T(8,128)(2,1)}, bf16[32,8192]{1,0:T(8,128)(2,1)S(1)}, u32[]{:S(2)}, u32[]{:S(2)}) collective-permute-start(bf16[32,8192]{1,0:T(8,128)(2,1)} %constant_dynamic-slice_fusion.24), channel_id=1, source_target_pairs={{24,16},{25,17},{26,18},{27,19},{28,20},{29,21},{30,22},{31,23}} | collective-permute-start | bytes 1572872 | tf_op jit(solution)/shard_map/ppermute | solution.py:27
  472.8 15.5 %collective-permute-start.47 = (bf16[128,2048]{1,0:T(8,128)(2,1)}, bf16[128,2048]{1,0:T(8,128)(2,1)S(1)}, u32[]{:S(2)}, u32[]{:S(2)}) collective-permute-start(bf16[128,2048]{1,0:T(8,128)(2,1)} %fusion.37), channel_id=1, source_target_pairs={{24,16},{25,17},{26,18},{27,19},{28,20},{29,21},{30,22},{31,23}} | collective-permute-start | bytes 1572872 | tf_op jit(solution)/shard_map/ppermute | solution.py:27
  489.5 7.6 collective-permute-start.48
  509.5 42.5 %collective-permute-start.59 = (f32[17,128]{1,0:T(8,128)S(1)}, f32[17,128]{1,0:T(8,128)S(1)}, u32[]{:S(2)}, u32[]{:S(2)}) collective-permute-start(f32[17,128]{1,0:T(8,128)S(1)} %fusion.161), channel_id=1, source_target_pairs={{16,22},{17,23},{18,16},{19,17},{20,18},{21,19},{22,20},{23,21}} | collective-permute-start | bytes 26120 | tf_op jit(solution)/shard_map/ppermute | solution.py:27
  552.0 7.0 collective-permute-start.58
  559.0 7.0 collective-permute-start.57
  583.1 31.9 %collective-permute-start.61 = (bf16[128,2048]{1,0:T(8,128)(2,1)S(1)}, bf16[128,2048]{1,0:T(8,128)(2,1)S(1)}, u32[]{:S(2)}, u32[]{:S(2)}) collective-permute-start(bf16[128,2048]{1,0:T(8,128)(2,1)S(1)} %fusion.34), channel_id=1, source_target_pairs={{16,9},{17,8},{18,11},{19,10},{20,13},{21,12},{22,15},{23,14}} | collective-permute-start | bytes 1572872 | tf_op jit(solution)/shard_map/ppermute | solution.py:27
  645.9 68.8 %collective-permute-done.73 = bf16[128,2048]{1,0:T(8,128)(2,1)S(1)} collective-permute-done((bf16[128,2048]{1,0:T(8,128)(2,1)}, bf16[128,2048]{1,0:T(8,128)(2,1)S(1)}, u32[]{:S(2)}, u32[]{:S(2)}) %collective-permute-start.73) | collective-permute-done | bytes 524320 | tf_op jit(solution)/shard_map/ppermute | solution.py:27
  736.8 29.2 %conditional.15 = (bf16[128,8192]{1,0:T(8,128)(2,1)}) conditional(s32[]{:T(128)} %convert_element_type.219, () %tuple.93, (bf16[128,4096]{1,0:T(8,128)(2,1)}, bf16[8192,4096]{1,0:T(8,128)(2,1)}) %tuple.94), branch_computations={%region_29.30_spmd, %region_30.31_spmd} | conditional | flops 8590983168 | bytes 70254600 | solution.py:195
  736.8 29.2 %convolution_convert_fusion.7 = bf16[128,8192]{1,0:T(8,128)(2,1)} fusion(bf16[128,4096]{1,0:T(8,128)(2,1)} %get-tuple-element.74, bf16[8192,4096]{1,0:T(8,128)(2,1)} %get-tuple-element.75), kind=kOutput, calls=%fused_computation.11 | convolution fusion | flops 8590983168 | bytes 70254592 | tf_op jit(solution)/shard_map/cond/branch_1_fun/dot_general | solution.py:188
  766.0 5.2 collective-permute-start.77
  778.0 18.4 %collective-permute-done.76 = bf16[128,2048]{1,0:T(8,128)(2,1)} collective-permute-done((bf16[128,2048]{1,0:T(8,128)(2,1)S(1)}, bf16[128,2048]{1,0:T(8,128)(2,1)}, u32[]{:S(2)}, u32[]{:S(2)}) %collective-permute-start.76) | collective-permute-done | bytes 524320 | tf_op jit(solution)/shard_map/ppermute | solution.py:27
  801.7 5.7 collective-permute-start.81
  818.3 11.2 %collective-permute-done.80 = bf16[128,2048]{1,0:T(8,128)(2,1)S(1)} collective-permute-done((bf16[128,2048]{1,0:T(8,128)(2,1)S(1)}, bf16[128,2048]{1,0:T(8,128)(2,1)S(1)}, u32[]{:S(2)}, u32[]{:S(2)}) %collective-permute-start.80) | collective-permute-done | bytes 524320 | tf_op jit(solution)/shard_map/ppermute | solution.py:27
  (407 shorter events, 248.9 us)
Async XLA Ops:
  0.6 71.4 %collective-permute-start.5 = (s32[4]{0:T(128)}, s32[4]{0:T(128)S(1)}, u32[]{:S(2)}, u32[]{:S(2)}) collective-permute-start(s32[4]{0:T(128)} %param.30), channel_id=1, source_target_pairs={{0,2},{2,4},{4,6},{6,0},{1,3},{3,5},{5,7},{7,1},{8,10},{10,12},{12... | collective-permute-start | bytes 56 | tf_op jit(solution)/shard_map/ppermute | solution.py:62
  7.8 67.2 %collective-permute-start.7 = (s32[4]{0:T(128)}, s32[4]{0:T(128)S(1)}, u32[]{:S(2)}, u32[]{:S(2)}) collective-permute-start(s32[4]{0:T(128)} %param.30), channel_id=1, source_target_pairs={{0,6},{2,0},{4,2},{6,4},{1,7},{3,1},{5,3},{7,5},{8,14},{10,8},{12,... | collective-permute-start | bytes 56 | tf_op jit(solution)/shard_map/ppermute | solution.py:62
  13.5 62.2 %collective-permute-start.6 = (s32[4]{0:T(128)}, s32[4]{0:T(128)S(1)}, u32[]{:S(2)}, u32[]{:S(2)}) collective-permute-start(s32[4]{0:T(128)} %param.30), channel_id=1, source_target_pairs={{0,4},{2,6},{4,0},{6,2},{1,5},{3,7},{5,1},{7,3},{8,12},{10,14},{12... | collective-permute-start | bytes 56 | tf_op jit(solution)/shard_map/ppermute | solution.py:62
  19.2 59.2 %collective-permute-start = (bf16[32,8192]{1,0:T(8,128)(2,1)}, bf16[32,8192]{1,0:T(8,128)(2,1)S(1)}, u32[]{:S(2)}, u32[]{:S(2)}) collective-permute-start(bf16[32,8192]{1,0:T(8,128)(2,1)} %param.24), channel_id=1, source_target_pairs={{0,2},{1,3},{2,4},{3,5},{4,6},{5,7},{6,0},{7,1}} | collective-permute-start | bytes 1572872 | tf_op jit(solution)/shard_map/ppermute | solution.py:27
  23.0 56.1 %collective-permute-start.2 = (bf16[32,8192]{1,0:T(8,128)(2,1)}, bf16[32,8192]{1,0:T(8,128)(2,1)S(1)}, u32[]{:S(2)}, u32[]{:S(2)}) collective-permute-start(bf16[32,8192]{1,0:T(8,128)(2,1)} %param.24), channel_id=1, source_target_pairs={{0,6},{1,7},{2,0},{3,1},{4,2},{5,3},{6,4},{7,5}} | collective-permute-start | bytes 1572872 | tf_op jit(solution)/shard_map/ppermute | solution.py:27
  93.0 38.1 %collective-permute-start.4 = (f32[1,128]{1,0:T(1,128)S(1)}, f32[1,128]{1,0:T(1,128)S(1)}, u32[]{:S(2)}, u32[]{:S(2)}) collective-permute-start(f32[1,128]{1,0:T(1,128)S(1)} %bitcast.448), channel_id=1, source_target_pairs={{0,1},{1,0},{2,3},{3,2},{4,5},{5,4},{6,7},{7,6}} | collective-permute-start | bytes 1544 | tf_op jit(solution)/shard_map/ppermute | solution.py:27
  171.9 60.8 %collective-permute-start.19 = (bf16[128,2048]{1,0:T(8,128)(2,1)S(1)}, bf16[128,2048]{1,0:T(8,128)(2,1)S(1)}, u32[]{:S(2)}, u32[]{:S(2)}) collective-permute-start(bf16[128,2048]{1,0:T(8,128)(2,1)S(1)} %get-tuple-element.207), channel_id=1, source_target_pairs={{8,22},{9,23},{10,16},{11,17},{12,18},{13,19},{14,20},{15,21}} | collective-permute-start | bytes 1572872 | tf_op jit(solution)/shard_map/ppermute | solution.py:27
  233.8 65.4 %collective-permute-start.21 = (f32[1,128]{1,0:T(1,128)S(1)}, f32[1,128]{1,0:T(1,128)S(1)}, u32[]{:S(2)}, u32[]{:S(2)}) collective-permute-start(f32[1,128]{1,0:T(1,128)S(1)} %bitcast.450), channel_id=1, source_target_pairs={{16,17},{17,16},{18,19},{19,18},{20,21},{21,20},{22,23},{23,22}} | collective-permute-start | bytes 1544 | tf_op jit(solution)/shard_map/ppermute | solution.py:27
  260.8 38.6 %collective-permute-start.20 = (bf16[128,2048]{1,0:T(8,128)(2,1)}, bf16[128,2048]{1,0:T(8,128)(2,1)S(1)}, u32[]{:S(2)}, u32[]{:S(2)}) collective-permute-start(bf16[128,2048]{1,0:T(8,128)(2,1)} %dynamic-slice_bitcast_fusion.21), channel_id=1, source_target_pairs={{16,17},{17,16},{18,19},{19,18},{20,21},{21,20},{22,23},{23,22}} | collective-permute-start | bytes 1572872 | tf_op jit(solution)/shard_map/ppermute | solution.py:27
  261.8 37.5 %collective-permute-start.22 = (f32[16,128]{1,0:T(8,128)S(1)}, f32[16,128]{1,0:T(8,128)S(1)}, u32[]{:S(2)}, u32[]{:S(2)}) collective-permute-start(f32[16,128]{1,0:T(8,128)S(1)} %bitcast.434), channel_id=1, source_target_pairs={{16,17},{17,16},{18,19},{19,18},{20,21},{21,20},{22,23},{23,22}} | collective-permute-start | bytes 24584 | tf_op jit(solution)/shard_map/ppermute | solution.py:27
  330.1 53.5 %collective-permute-start.28 = (f32[1,128]{1,0:T(1,128)S(1)}, f32[1,128]{1,0:T(1,128)S(1)}, u32[]{:S(2)}, u32[]{:S(2)}) collective-permute-start(f32[1,128]{1,0:T(1,128)S(1)} %bitcast.447), channel_id=1, source_target_pairs={{24,25},{25,24},{26,27},{27,26},{28,29},{29,28},{30,31},{31,30}} | collective-permute-start | bytes 1544 | tf_op jit(solution)/shard_map/ppermute | solution.py:27
  334.5 49.3 %collective-permute-start.27 = (bf16[128,2048]{1,0:T(8,128)(2,1)S(1)}, bf16[128,2048]{1,0:T(8,128)(2,1)}, u32[]{:S(2)}, u32[]{:S(2)}) collective-permute-start(bf16[128,2048]{1,0:T(8,128)(2,1)S(1)} %dynamic-slice_bitcast_fusion.16), channel_id=1, source_target_pairs={{24,25},{25,24},{26,27},{27,26},{28,29},{29,28},{30,31},{31,30}} | collective-permute-start | bytes 1572872 | tf_op jit(solution)/shard_map/ppermute | solution.py:27
  336.3 47.4 %collective-permute-start.29 = (f32[16,128]{1,0:T(8,128)S(1)}, f32[16,128]{1,0:T(8,128)S(1)}, u32[]{:S(2)}, u32[]{:S(2)}) collective-permute-start(f32[16,128]{1,0:T(8,128)S(1)} %bitcast.431), channel_id=1, source_target_pairs={{24,25},{25,24},{26,27},{27,26},{28,29},{29,28},{30,31},{31,30}} | collective-permute-start | bytes 24584 | tf_op jit(solution)/shard_map/ppermute | solution.py:27
  405.1 63.6 %collective-permute-start.42 = (bf16[128,2048]{1,0:T(8,128)(2,1)}, bf16[128,2048]{1,0:T(8,128)(2,1)}, u32[]{:S(2)}, u32[]{:S(2)}) collective-permute-start(bf16[128,2048]{1,0:T(8,128)(2,1)} %get-tuple-element.154), channel_id=1, source_target_pairs={{24,30},{25,31},{26,24},{27,25},{28,26},{29,27},{30,28},{31,29}} | collective-permute-start | bytes 1572872 | tf_op jit(solution)/shard_map/ppermute | solution.py:27
  406.6 62.1 %collective-permute-start.41 = (bf16[128,2048]{1,0:T(8,128)(2,1)S(1)}, bf16[128,2048]{1,0:T(8,128)(2,1)}, u32[]{:S(2)}, u32[]{:S(2)}) collective-permute-start(bf16[128,2048]{1,0:T(8,128)(2,1)S(1)} %get-tuple-element.155), channel_id=1, source_target_pairs={{24,28},{25,29},{26,30},{27,31},{28,24},{29,25},{30,26},{31,27}} | collective-permute-start | bytes 1572872 | tf_op jit(solution)/shard_map/ppermute | solution.py:27
  408.8 79.6 %collective-permute-start.35 = (bf16[32,8192]{1,0:T(8,128)(2,1)}, bf16[32,8192]{1,0:T(8,128)(2,1)S(1)}, u32[]{:S(2)}, u32[]{:S(2)}) collective-permute-start(bf16[32,8192]{1,0:T(8,128)(2,1)} %constant_dynamic-slice_fusion.22), channel_id=1, source_target_pairs={{8,0},{9,1},{10,2},{11,3},{12,4},{13,5},{14,6},{15,7}} | collective-permute-start | bytes 1572872 | tf_op jit(solution)/shard_map/ppermute | solution.py:27
  410.3 78.1 %collective-permute-start.34 = (bf16[32,8192]{1,0:T(8,128)(2,1)}, bf16[32,8192]{1,0:T(8,128)(2,1)S(1)}, u32[]{:S(2)}, u32[]{:S(2)}) collective-permute-start(bf16[32,8192]{1,0:T(8,128)(2,1)} %constant_dynamic-slice_fusion.23), channel_id=1, source_target_pairs={{16,8},{17,9},{18,10},{19,11},{20,12},{21,13},{22,14},{23,15}} | collective-permute-start | bytes 1572872 | tf_op jit(solution)/shard_map/ppermute | solution.py:27
  412.1 76.3 %collective-permute-start.33 = (bf16[32,8192]{1,0:T(8,128)(2,1)}, bf16[32,8192]{1,0:T(8,128)(2,1)S(1)}, u32[]{:S(2)}, u32[]{:S(2)}) collective-permute-start(bf16[32,8192]{1,0:T(8,128)(2,1)} %constant_dynamic-slice_fusion.24), channel_id=1, source_target_pairs={{24,16},{25,17},{26,18},{27,19},{28,20},{29,21},{30,22},{31,23}} | collective-permute-start | bytes 1572872 | tf_op jit(solution)/shard_map/ppermute | solution.py:27
  503.2 55.8 %collective-permute-start.51 = (bf16[128,2048]{1,0:T(8,128)(2,1)S(1)}, bf16[128,2048]{1,0:T(8,128)(2,1)S(1)}, u32[]{:S(2)}, u32[]{:S(2)}) collective-permute-start(bf16[128,2048]{1,0:T(8,128)(2,1)S(1)} %collective-permute-done.47), channel_id=1, source_target_pairs={{16,22},{17,23},{18,16},{19,17},{20,18},{21,19},{22,20},{23,21}} | collective-permute-start | bytes 1572872 | tf_op jit(solution)/shard_map/ppermute | solution.py:27
  503.9 62.2 %collective-permute-start.50 = (bf16[128,2048]{1,0:T(8,128)(2,1)S(1)}, bf16[128,2048]{1,0:T(8,128)(2,1)}, u32[]{:S(2)}, u32[]{:S(2)}) collective-permute-start(bf16[128,2048]{1,0:T(8,128)(2,1)S(1)} %collective-permute-done.47), channel_id=1, source_target_pairs={{16,20},{17,21},{18,22},{19,23},{20,16},{21,17},{22,18},{23,19}} | collective-permute-start | bytes 1572872 | tf_op jit(solution)/shard_map/ppermute | solution.py:27
  505.4 60.7 %collective-permute-start.49 = (bf16[128,2048]{1,0:T(8,128)(2,1)S(1)}, bf16[128,2048]{1,0:T(8,128)(2,1)}, u32[]{:S(2)}, u32[]{:S(2)}) collective-permute-start(bf16[128,2048]{1,0:T(8,128)(2,1)S(1)} %collective-permute-done.47), channel_id=1, source_target_pairs={{16,18},{17,19},{18,20},{19,21},{20,22},{21,23},{22,16},{23,17}} | collective-permute-start | bytes 1572872 | tf_op jit(solution)/shard_map/ppermute | solution.py:27
  509.5 64.6 %collective-permute-start.59 = (f32[17,128]{1,0:T(8,128)S(1)}, f32[17,128]{1,0:T(8,128)S(1)}, u32[]{:S(2)}, u32[]{:S(2)}) collective-permute-start(f32[17,128]{1,0:T(8,128)S(1)} %fusion.161), channel_id=1, source_target_pairs={{16,22},{17,23},{18,16},{19,17},{20,18},{21,19},{22,20},{23,21}} | collective-permute-start | bytes 26120 | tf_op jit(solution)/shard_map/ppermute | solution.py:27
  578.9 36.0 %collective-permute-start.60 = (bf16[128,2048]{1,0:T(8,128)(2,1)S(1)}, bf16[128,2048]{1,0:T(8,128)(2,1)S(1)}, u32[]{:S(2)}, u32[]{:S(2)}) collective-permute-start(bf16[128,2048]{1,0:T(8,128)(2,1)S(1)} %fusion.34), channel_id=1, source_target_pairs={{16,8},{17,9},{18,10},{19,11},{20,12},{21,13},{22,14},{23,15}} | collective-permute-start | bytes 1572872 | tf_op jit(solution)/shard_map/ppermute | solution.py:27
  581.5 266.6 %collective-permute-start.52 = (bf16[32,8192]{1,0:T(8,128)(2,1)}, bf16[32,8192]{1,0:T(8,128)(2,1)}, u32[]{:S(2)}, u32[]{:S(2)}) collective-permute-start(bf16[32,8192]{1,0:T(8,128)(2,1)} %constant_dynamic-slice_fusion.16), channel_id=1, source_target_pairs={{16,24},{17,25},{18,26},{19,27},{20,28},{21,29},{22,30},{23,31}} | collective-permute-start | bytes 1572872 | tf_op jit(solution)/shard_map/ppermute | solution.py:27
  583.1 35.4 %collective-permute-start.61 = (bf16[128,2048]{1,0:T(8,128)(2,1)S(1)}, bf16[128,2048]{1,0:T(8,128)(2,1)S(1)}, u32[]{:S(2)}, u32[]{:S(2)}) collective-permute-start(bf16[128,2048]{1,0:T(8,128)(2,1)S(1)} %fusion.34), channel_id=1, source_target_pairs={{16,9},{17,8},{18,11},{19,10},{20,13},{21,12},{22,15},{23,14}} | collective-permute-start | bytes 1572872 | tf_op jit(solution)/shard_map/ppermute | solution.py:27
  640.0 74.7 %collective-permute-start.73 = (bf16[128,2048]{1,0:T(8,128)(2,1)}, bf16[128,2048]{1,0:T(8,128)(2,1)S(1)}, u32[]{:S(2)}, u32[]{:S(2)}) collective-permute-start(bf16[128,2048]{1,0:T(8,128)(2,1)} %fusion.31), channel_id=1, source_target_pairs={{8,0},{9,1},{10,2},{11,3},{12,4},{13,5},{14,6},{15,7}} | collective-permute-start | bytes 1572872 | tf_op jit(solution)/shard_map/ppermute | solution.py:27
  643.1 204.9 %collective-permute-start.65 = (bf16[32,8192]{1,0:T(8,128)(2,1)}, bf16[32,8192]{1,0:T(8,128)(2,1)}, u32[]{:S(2)}, u32[]{:S(2)}) collective-permute-start(bf16[32,8192]{1,0:T(8,128)(2,1)} %constant_dynamic-slice_fusion.12), channel_id=1, source_target_pairs={{8,16},{9,17},{10,18},{11,19},{12,20},{13,21},{14,22},{15,23}} | collective-permute-start | bytes 1572872 | tf_op jit(solution)/shard_map/ppermute | solution.py:27
  644.6 81.2 %collective-permute-start.74 = (bf16[128,2048]{1,0:T(8,128)(2,1)}, bf16[128,2048]{1,0:T(8,128)(2,1)}, u32[]{:S(2)}, u32[]{:S(2)}) collective-permute-start(bf16[128,2048]{1,0:T(8,128)(2,1)} %fusion.31), channel_id=1, source_target_pairs={{8,1},{9,0},{10,3},{11,2},{12,5},{13,4},{14,7},{15,6}} | collective-permute-start | bytes 1572872 | tf_op jit(solution)/shard_map/ppermute | solution.py:27
  727.2 38.8 %collective-permute-start.85 = (f32[17,128]{1,0:T(8,128)S(1)}, f32[17,128]{1,0:T(8,128)S(1)}, u32[]{:S(2)}, u32[]{:S(2)}) collective-permute-start(f32[17,128]{1,0:T(8,128)S(1)} %fusion.159), channel_id=1, source_target_pairs={{0,6},{1,7},{2,0},{3,1},{4,2},{5,3},{6,4},{7,5}} | collective-permute-start | bytes 26120 | tf_op jit(solution)/shard_map/ppermute | solution.py:27
  731.3 39.9 %collective-permute-start.84 = (f32[17,128]{1,0:T(8,128)S(1)}, f32[17,128]{1,0:T(8,128)S(1)}, u32[]{:S(2)}, u32[]{:S(2)}) collective-permute-start(f32[17,128]{1,0:T(8,128)S(1)} %fusion.159), channel_id=1, source_target_pairs={{0,4},{1,5},{2,6},{3,7},{4,0},{5,1},{6,2},{7,3}} | collective-permute-start | bytes 26120 | tf_op jit(solution)/shard_map/ppermute | solution.py:27
  733.2 41.1 %collective-permute-start.83 = (f32[17,128]{1,0:T(8,128)S(1)}, f32[17,128]{1,0:T(8,128)S(1)}, u32[]{:S(2)}, u32[]{:S(2)}) collective-permute-start(f32[17,128]{1,0:T(8,128)S(1)} %fusion.159), channel_id=1, source_target_pairs={{0,2},{1,3},{2,4},{3,5},{4,6},{5,7},{6,0},{7,1}} | collective-permute-start | bytes 26120 | tf_op jit(solution)/shard_map/ppermute | solution.py:27
  771.2 25.2 %collective-permute-start.76 = (bf16[128,2048]{1,0:T(8,128)(2,1)S(1)}, bf16[128,2048]{1,0:T(8,128)(2,1)}, u32[]{:S(2)}, u32[]{:S(2)}) collective-permute-start(bf16[128,2048]{1,0:T(8,128)(2,1)S(1)} %collective-permute-done.73), channel_id=1, source_target_pairs={{0,4},{1,5},{2,6},{3,7},{4,0},{5,1},{6,2},{7,3}} | collective-permute-start | bytes 1572872 | tf_op jit(solution)/shard_map/ppermute | solution.py:27
  (98 other events, 1700.9 us)
